TPU v7x, 32 devices: a whole 2x2x4 slice. The times are simulated.
32 devices in a mesh: tower: 2 (over y), dp: 16 (over z, x, core).
Axes of the slice: x: 2, y: 2, z: 4, core: 2. Of those that a mesh axis runs over, the one named last changes fastest.
Arguments:
- hidden_in: bfloat16 [2, 8192, 768], P('tower', 'dp'), may hold values from -6 to 6
- seg_ids: int32 [16, 512], P('dp'), may hold values from 0 to 3, never falling along the last dimension, each value on 1 to 320 neighbouring positions
- labels: int32 [256], P('dp'), may hold values from 0 to 63
- out_grad: bfloat16 [2, 8192, 768], P('tower', 'dp'), may hold values from -2 to 2
- w_qkv: bfloat16 [2, 768, 2304], P('tower'), may hold values from -0.3125 to 0.3125
- b_query: float32 [2, 768], P('tower'), may hold values from -3 to 3
- b_value: float32 [2, 768], P('tower'), may hold values from -3 to 3
- w_out: bfloat16 [2, 768, 768], P('tower'), may hold values from -0.625 to 0.625
- b_out: float32 [2, 768], P('tower'), may hold values from -3 to 3
- ln1_gain: float32 [2, 768], P('tower'), may hold values from 0.5 to 1.5
- ln1_bias: float32 [2, 768], P('tower'), may hold values from -2 to 2
- w_in: bfloat16 [2, 768, 3072], P('tower'), may hold values from -0.21875 to 0.21875
- b_in: float32 [2, 3072], P('tower'), may hold values from -3 to 3
- w_back: bfloat16 [2, 3072, 768], P('tower'), may hold values from -0.109375 to 0.109375
- b_back: float32 [2, 768], P('tower'), may hold values from -3 to 3
- ln2_gain: float32 [2, 768], P('tower'), may hold values from 0.5 to 1.5
- ln2_bias: float32 [2, 768], P('tower'), may hold values from -2 to 2
Outputs:
- out_hidden: bfloat16 [2, 8192, 768], P('tower', 'dp')
- grad_hidden: bfloat16 [2, 8192, 768], P('tower', 'dp')
- grad_w_qkv: float32 [2, 768, 2304], P('tower', 'dp')
- grad_b_query: float32 [2, 768], P('tower', 'dp')
- grad_b_value: float32 [2, 768], P('tower', 'dp')
- grad_w_out: float32 [2, 768, 768], P('tower', 'dp')
- grad_b_out: float32 [2, 768], P('tower', 'dp')
- grad_ln1_gain: float32 [2, 768], P('tower', 'dp')
- grad_ln1_bias: float32 [2, 768], P('tower', 'dp')
- grad_w_in: float32 [2, 768, 3072], P('tower', 'dp')
- grad_b_in: float32 [2, 3072], P('tower', 'dp')
- grad_w_back: float32 [2, 3072, 768], P('tower', 'dp')
- grad_b_back: float32 [2, 768], P('tower', 'dp')
- grad_ln2_gain: float32 [2, 768], P('tower', 'dp')
- grad_ln2_bias: float32 [2, 768], P('tower', 'dp')
Inputs may be any that keep to these rules, and one draw needn't show every extreme that they name: `seg_ids`: each row holds 4 passages in order, each 1 to 320 tokens long, and one passage of each row has exactly 320.
All inputs are finite; a program needn't handle non-finite values.
Results may differ from a plain program's by a relative error of at most 0.014.
The roundings to bfloat16 on the way count: a program that leaves them out, or rounds other values in their place, can miss the bound.
Values may be sent and summed in bfloat16 or wider, within the bound.
No kernel may reach another device: no remote copies, remote signals or barrier semaphores. Data moves between devices by JAX's collectives and lax.ppermute only.
A program may use at most 192 MiB of HBM per device.

v0:
```python
import functools
import math

import jax
import jax.numpy as jnp
from jax import lax
from jax.experimental import pallas as pl
from jax.experimental.pallas import tpu as pltpu
from jax.sharding import PartitionSpec as P

HEAD_DIM = 64
QLEN = 32
SEGS = 4
PACKET = 24
EPS = 1e-05
BF = jnp.bfloat16
F32 = jnp.float32
TILE = 32

COSTS = {"first_back": 3 * 10**10, "attention_back_4": 3 * 10**10, "input_back": 3 * 10**10}

VM = pl.BlockSpec(memory_space=pltpu.VMEM)
SM = pl.BlockSpec(memory_space=pltpu.SMEM)
HB = pl.BlockSpec(memory_space=pltpu.HBM)


def nn(a, b):
    return lax.dot_general(a, b, (((1,), (0,)), ((), ())), preferred_element_type=F32)


def nt(a, b):
    return lax.dot_general(a, b, (((1,), (1,)), ((), ())), preferred_element_type=F32)


def tn(a, b):
    return lax.dot_general(a, b, (((0,), (0,)), ((), ())), preferred_element_type=F32)


def kernel_call(body, outs, args, scratch=(), smem=0, hbm=0, mib=32, flops=0, name=None):
    single = not isinstance(outs, (list, tuple))
    shapes = [outs] if single else list(outs)
    result = pl.pallas_call(
        body,
        out_shape=shapes,
        in_specs=[SM] * smem + [VM] * (len(args) - smem - hbm) + [HB] * hbm,
        out_specs=[VM] * len(shapes),
        scratch_shapes=list(scratch),
        compiler_params=pltpu.CompilerParams(vmem_limit_bytes=mib << 20),
        cost_estimate=pl.CostEstimate(flops=COSTS.get(name, 0), bytes_accessed=0, transcendentals=0),
        name=name,
    )(*args)
    return result[0] if single else result


def sds(shape, dtype):
    return jax.ShapeDtypeStruct(shape, dtype)


def fold(value):
    rows, cols = value.shape
    return jnp.sum(value.reshape(rows // 8, 8, cols), 0)


def head_mask(half):
    lane = lax.broadcasted_iota(jnp.int32, (1, 2 * HEAD_DIM), 1)
    return (lane // HEAD_DIM == half).astype(F32).astype(BF)


def normalise(value):
    centred = value - jnp.mean(value, -1, keepdims=True)
    inverse = lax.rsqrt(jnp.mean(centred * centred, -1, keepdims=True) + EPS)
    return centred * inverse, inverse


def norm_back(grad, normed, inverse, gain):
    scaled = grad * gain
    return inverse * (
        scaled
        - jnp.mean(scaled, -1, keepdims=True)
        - normed * jnp.mean(scaled * normed, -1, keepdims=True)
    )


def gelu_pair(value):
    cdf = 0.5 * lax.erf(value * (1.0 / math.sqrt(2.0))) + 0.5
    density = jnp.exp(value * value * -0.5) * (1.0 / math.sqrt(2.0 * math.pi))
    return value * cdf, cdf + value * density


def proj_kernel(x_hbm, w_hbm, bq_hbm, bv_hbm, out, x, w0, w1, w2, bq, bv, sems):
    width = x.shape[1]
    parts = (w0, w1, w2)
    copies = [
        pltpu.make_async_copy(w_hbm.at[:, pl.ds(k * width, width)], parts[k], sems.at[k]) for k in range(3)
    ]
    x_copy = pltpu.make_async_copy(x_hbm, x, sems.at[3])
    bq_copy = pltpu.make_async_copy(bq_hbm, bq, sems.at[4])
    bv_copy = pltpu.make_async_copy(bv_hbm, bv, sems.at[5])
    for copy in (x_copy, copies[1], copies[0], bq_copy, copies[2], bv_copy):
        copy.start()
    x_copy.wait()
    for k in (1, 0, 2):
        copies[k].wait()
        value = nn(x[...], parts[k][...])
        if k == 0:
            bq_copy.wait()
            value = value + bq[...]
        if k == 2:
            bv_copy.wait()
            value = value + bv[...]
        out[:, k * width : (k + 1) * width] = value.astype(BF)


def chosen_rows(tower, seg, count, length):
    row = lax.broadcasted_iota(jnp.int32, (count, 1), 0)
    place = lax.broadcasted_iota(jnp.int32, (count, length), 1)
    start = jnp.sum((seg < row).astype(F32), 1, keepdims=True).astype(jnp.int32)
    wanted = jnp.where(tower == 0, row * QLEN, jnp.where(row < SEGS, start, -1))
    return (place == wanted).astype(F32)


def cls_kernel(place, seg, x, proj, w_out, b_out, g1, b1, w_in, b_in, w_back, b_back, g2, b2, cls):
    length, width = x.shape
    count = cls.shape[0]
    heads = width // HEAD_DIM
    tower = place[0]
    pick = chosen_rows(tower, seg[...], count, length)
    pick_low = pick.astype(BF)
    x_cls = nn(pick_low, x[...])
    q_cls = (nn(pick_low, proj[:, :width]) * (1.0 / math.sqrt(HEAD_DIM))).astype(BF)
    place_row = lax.broadcasted_iota(jnp.int32, (1, length), 1)
    own_seg = jnp.where(tower == 0, place_row // QLEN, seg[...])
    row = lax.broadcasted_iota(jnp.int32, (count, 1), 0)
    bias = jnp.where(own_seg == row, 0.0, -1e9)
    lane_head = lax.broadcasted_iota(jnp.int32, (1, width), 1) // HEAD_DIM
    spread = jnp.concatenate(
        [q_cls * (lane_head == h).astype(F32).astype(BF) for h in range(heads)], 0
    )
    scores = nt(spread, proj[:, width : 2 * width]) + jnp.concatenate([bias] * heads, 0)
    shifted = jnp.exp(scores - jnp.max(scores, -1, keepdims=True))
    probs = (shifted / jnp.sum(shifted, -1, keepdims=True)).astype(BF)
    mixed = nn(probs, proj[:, 2 * width :])
    attended = jnp.zeros((count, width), F32)
    for h in range(heads):
        attended = attended + jnp.where(lane_head == h, mixed[h * count : (h + 1) * count], 0.0)
    first = x_cls + (nn(attended.astype(BF), w_out[...]) + b_out[...])
    normed = normalise(first)[0] * g1[...] + b1[...]
    inner = nn(normed.astype(BF), w_in[...]) + b_in[...]
    act = gelu_pair(inner)[0].astype(BF)
    second = normed + (nn(act, w_back[...]) + b_back[...])
    final = normalise(second)[0] * g2[...] + b2[...]
    cls[...] = final.astype(BF)


def attention_kernel(place, seg_row, seg_col, proj, attended, probs, bias, *work):
    length = proj.shape[0]
    width = proj.shape[1] // 3
    tower = place[0]
    lane = lax.broadcasted_iota(jnp.int32, (1, length), 1)
    sub = lax.broadcasted_iota(jnp.int32, (length, 1), 0)
    row_seg = jnp.where(tower == 0, lane // QLEN, seg_row[...])
    col_seg = jnp.where(tower == 0, sub // QLEN, seg_col[...])
    bias[...] = jnp.where(col_seg == row_seg, 0.0, -1e9)
    masks = [head_mask(0), head_mask(1)]
    scale = jnp.asarray(1.0 / math.sqrt(HEAD_DIM), BF)
    step = 2 * HEAD_DIM
    pairs = width // step
    work_a, work_b = work

    def columns(part, pair):
        return proj[:, pl.ds(pl.multiple_of(part * width + pair * step, step), step)]

    def scores(pair, ref):
        queries, keys = columns(0, pair) * scale, columns(1, pair)
        for half in range(2):
            ref[half] = nt(queries * masks[half], keys)

    def soften(pair, ref):
        for half in range(2):
            for r in range(0, length, TILE):
                value = ref[half, r : r + TILE, :] + bias[r : r + TILE, :]
                shifted = jnp.exp(value - jnp.max(value, -1, keepdims=True))
                total = jnp.sum(shifted, -1, keepdims=True)
                probs[2 * pair + half, r : r + TILE, :] = (shifted * (1.0 / total)).astype(BF)

    def mix(pair):
        values = columns(2, pair)
        mixed = nn(probs[2 * pair], values * masks[0]) + nn(probs[2 * pair + 1], values * masks[1])
        attended[:, pl.ds(pl.multiple_of(pair * step, step), step)] = mixed.astype(BF)

    def two_pairs(k, carry):
        pair = 2 * k
        scores(pair + 1, work_b)
        soften(pair, work_a)
        scores(jnp.minimum(pair + 2, pairs - 1), work_a)
        mix(pair)
        soften(pair + 1, work_b)
        mix(pair + 1)
        return carry

    scores(0, work_a)
    lax.fori_loop(0, pairs // 2, two_pairs, 0)


def first_kernel(x, attended, w_out, b_out, g1, b1, n1, r1, low, work):
    work[...] = nn(attended[...], w_out[...])
    def step(i, carry):
        rows = pl.ds(pl.multiple_of(i * TILE, TILE), TILE)
        first = x[rows, :].astype(F32) + (work[rows, :] + b_out[...])
        normed, inverse = normalise(first)
        n1[rows, :] = normed
        r1[rows, :] = inverse
        low[rows, :] = (normed * g1[...] + b1[...]).astype(BF)
        return carry

    lax.fori_loop(0, x.shape[0] // TILE, step, 0, unroll=4)


def inner_kernel(low, w_in, b_in, act, slope, work_a, work_b):
    length = low.shape[0]
    block = work_a.shape[1]
    blocks = w_in.shape[1] // block

    def columns(i):
        return pl.ds(pl.multiple_of(i * block, block), block)

    def gelu_block(i, work):
        bias = b_in[:, columns(i)]
        for r in range(0, length, TILE):
            value, grad = gelu_pair(work[r : r + TILE, :] + bias)
            act[r : r + TILE, columns(i)] = value.astype(BF)
            slope[r : r + TILE, columns(i)] = grad.astype(BF)

    work_a[...] = nn(low[...], w_in[:, :block])

    def step(k, carry):
        i = 2 * k
        work_b[...] = nn(low[...], w_in[:, columns(i + 1)])
        gelu_block(i, work_a)
        work_a[...] = nn(low[...], w_in[:, columns(jnp.minimum(i + 2, blocks - 1))])
        gelu_block(i + 1, work_b)
        return carry

    lax.fori_loop(0, blocks // 2, step, 0)


def second_kernel(act, w_back, b_back, n1, g1, b1, g2, b2, n2, r2, out, work):
    part = work.shape[0]

    def normalise_part(k, carry):
        at = pl.multiple_of(k * part, part)
        work[...] = nn(act[pl.ds(at, part), :], w_back[...])
        for r in range(0, part, TILE):
            rows = pl.ds(pl.multiple_of(at + r, TILE), TILE)
            branch = work[r : r + TILE, :] + b_back[...]
            second = (n1[rows, :] * g1[...] + b1[...]) + branch
            normed, inverse = normalise(second)
            n2[rows, :] = normed
            r2[rows, :] = inverse
            out[rows, :] = (normed * g2[...] + b2[...]).astype(BF)
        return carry

    lax.fori_loop(0, act.shape[0] // part, normalise_part, 0)


def packet_kernel(place, cls, other, labels, out):
    query = place[0] == 0
    count, width = cls.shape
    mine, came = cls[...].astype(F32), other[...].astype(F32)
    q_rows = jnp.where(query, mine, came)
    p_rows = jnp.where(query, came, mine)[:SEGS]
    value = labels[...]
    gap = jnp.zeros((1, 128 - count), F32)
    row = jnp.concatenate(
        [(value >> 8).astype(F32), gap, (value & 255).astype(F32), gap, jnp.zeros((1, width - 256), F32)], 1
    )
    rest = jnp.zeros((PACKET - count - SEGS - 1, width), F32)
    out[...] = jnp.concatenate([q_rows, p_rows, row, rest], 0).astype(BF)


def loss_kernel(place, near, far, grad, *, order, count):
    tower, me = place[0], place[1]
    packets = jnp.concatenate([near[...], far[...]], 0)
    total, width = packets.shape
    scale = 2.0 / math.sqrt(width)
    row = lax.broadcasted_iota(jnp.int32, (total, 1), 0)
    col = lax.broadcasted_iota(jnp.int32, (1, total), 1)
    col_slot, col_part = col // PACKET, col % PACKET
    mixed = jnp.zeros_like(col)
    for j, b in enumerate(order):
        mixed = mixed | (((col_slot >> j) & 1) << b)
    is_passage = jnp.logical_and(col_part >= count, col_part < count + SEGS)
    number = jnp.where(is_passage, (mixed ^ me) * SEGS + (col_part - count), -1)
    label_of = ((row // PACKET) * PACKET + (count + SEGS) == col).astype(F32).astype(BF)
    label_rows = nn(label_of, packets[:, :256])
    lane = lax.broadcasted_iota(jnp.int32, (1, 256), 1)
    part = row % PACKET
    weight = jnp.where(lane == part, 256.0, 0.0) + jnp.where(lane == part + 128, 1.0, 0.0)
    label = jnp.sum(label_rows * weight, 1, keepdims=True).astype(jnp.int32)
    logits = jnp.where(is_passage, nt(packets, packets) * scale, -1e30)
    soft = jnp.exp(logits - jnp.max(logits, -1, keepdims=True))
    soft = soft / jnp.sum(soft, -1, keepdims=True)
    grad_logits = soft - (number == label).astype(F32)
    grad_logits = grad_logits * (part < count).astype(F32)
    wide = packets.astype(F32)
    grad_q = jnp.dot(
        grad_logits[:count], wide, precision=lax.Precision.HIGHEST, preferred_element_type=F32
    )
    pick = lax.broadcasted_iota(jnp.int32, (count, 1), 0)
    pick = jnp.logical_and(pick + count == col, pick < SEGS).astype(F32)
    turned = lax.dot_general(
        pick, grad_logits, (((1,), (1,)), ((), ())),
        precision=lax.Precision.HIGHEST, preferred_element_type=F32,
    )
    grad_p = jnp.dot(turned, wide, precision=lax.Precision.HIGHEST, preferred_element_type=F32)
    grad[...] = jnp.where(tower == 0, grad_q, grad_p) * scale


def plain_loss(packets, tower, me, count):
    devices, _, width = packets.shape
    scale = 2.0 / math.sqrt(width)
    queries = packets[:, :count].reshape(devices * count, width)
    passages = packets[:, count : count + SEGS].reshape(devices * SEGS, width)
    row = packets[:, count + SEGS].astype(jnp.int32)
    label = (row[:, :count] * 256 + row[:, 128 : 128 + count]).reshape(devices * count, 1)
    soft = jax.nn.softmax(nt(queries, passages) * scale, -1)
    grad = soft - (label == jnp.arange(devices * SEGS, dtype=jnp.int32)).astype(F32)
    grad_q = lax.dynamic_slice_in_dim(grad, me * count, count, 0)
    grad_q = jnp.dot(grad_q, passages.astype(F32), precision=lax.Precision.HIGHEST)
    grad_p = lax.dynamic_slice_in_dim(grad, me * SEGS, SEGS, 1)
    grad_p = jnp.dot(grad_p.T, queries.astype(F32), precision=lax.Precision.HIGHEST)
    grad_p = jnp.pad(grad_p, ((0, count - SEGS), (0, 0)))
    return jnp.where(tower == 0, grad_q, grad_p) * scale


def split_three(value):
    high = value.astype(BF)
    rest = value - high.astype(F32)
    middle = rest.astype(BF)
    return jnp.concatenate([high, middle, (rest - middle.astype(F32)).astype(BF)], 0)


def norm_back_rows(rows, grad, normed, inverse, gain, out, low, totals):
    back = norm_back(grad, normed[rows, :], inverse[rows, :], gain[...])
    out[rows, :] = back
    back_low = back.astype(BF)
    low[rows, :] = back_low
    parts = (fold(grad * normed[rows, :]), fold(grad), fold(back_low.astype(F32)))
    return parts if totals is None else tuple(a + b for a, b in zip(totals, parts))


def second_back_kernel(place, seg, out_grad, cls_grad, n2, r2, g2, grad, low, sums, work):
    length, width = out_grad.shape
    count = cls_grad.shape[0]
    pick = chosen_rows(place[0], seg[...], count, length).astype(BF)
    work[...] = tn(jnp.concatenate([pick] * 3, 0), split_three(cls_grad[...]))
    totals = None
    for r in range(0, length, TILE):
        rows = slice(r, r + TILE)
        final = out_grad[rows, :].astype(F32) + work[rows, :]
        totals = norm_back_rows(rows, final, n2, r2, g2, grad, low, totals)
    for k, part in enumerate(totals):
        sums[k : k + 1, :] = jnp.sum(part, 0, keepdims=True)


def inner_back_kernel(low, w_back, slope, out, sums):
    block = 256

    def step(i, carry):
        cols = pl.ds(pl.multiple_of(i * block, block), block)
        value = (nt(low[...], w_back[cols, :]) * slope[:, cols].astype(F32)).astype(BF)
        out[:, cols] = value
        sums[:, cols] = jnp.sum(value.astype(F32), 0, keepdims=True)
        return carry

    lax.fori_loop(0, w_back.shape[0] // block, step, 0, unroll=2)


def first_back_kernel(inner, w_in, grad_second, n1, r1, g1, w_out, grad, low, att, sums, work):
    length, width = grad_second.shape
    part = work.shape[0]

    def back_part(k, totals):
        at = pl.multiple_of(k * part, part)
        work[...] = nt(inner[pl.ds(at, part), :], w_in[...])
        for r in range(0, part, TILE):
            rows = pl.ds(pl.multiple_of(at + r, TILE), TILE)
            value = grad_second[rows, :] + work[r : r + TILE, :]
            totals = norm_back_rows(rows, value, n1, r1, g1, grad, low, totals)
        rows = pl.ds(at, part)
        att[rows, :] = nt(low[rows, :], w_out[...]).astype(BF)
        return totals

    zero = jnp.zeros((8, width), F32)
    totals = lax.fori_loop(0, length // part, back_part, (zero, zero, zero))
    for k, total in enumerate(totals):
        sums[k : k + 1, :] = jnp.sum(total, 0, keepdims=True)


def attention_back_kernel(proj, probs, att_grad, out, sums, dp_a, dp_b, ds_a, ds_b, *, first):
    length = proj.shape[0]
    width = proj.shape[1] // 3
    own = out.shape[1] // 3
    masks = [head_mask(0), head_mask(1)]
    scale = 1.0 / math.sqrt(HEAD_DIM)
    step = 2 * HEAD_DIM
    pairs = own // step

    def columns(part, pair):
        return proj[:, pl.ds(pl.multiple_of(part * width + (first + pair) * step, step), step)]

    def grad_columns(pair):
        return att_grad[:, pl.ds(pl.multiple_of((first + pair) * step, step), step)]

    def grad_probs(pair, dp):
        grads, values = grad_columns(pair), columns(2, pair)
        for half in range(2):
            dp[half] = nt(grads * masks[half], values)

    def grad_scores(pair, dp, ds):
        for half in range(2):
            for r in range(0, length, TILE):
                wide = probs[2 * (first + pair) + half, r : r + TILE, :].astype(F32)
                grad = dp[half, r : r + TILE, :]
                delta = jnp.sum(grad * wide, -1, keepdims=True)
                ds[half, r : r + TILE, :] = (wide * (grad - delta)).astype(BF)

    def results(pair, ds):
        queries_t, grads_t = columns(0, pair).T, grad_columns(pair).T
        keys = columns(1, pair)
        grad_q, grad_k_t, grad_v_t = None, [], []
        for half in range(2):
            scores = ds[half]
            lanes = slice(half * HEAD_DIM, (half + 1) * HEAD_DIM)
            grad_v_t.append(nn(grads_t[lanes], probs[2 * (first + pair) + half]))
            grad_k_t.append(nn(queries_t[lanes], scores))
            term = nn(scores, keys * masks[half])
            grad_q = term if grad_q is None else grad_q + term
        parts = (
            grad_q * scale,
            jnp.concatenate(grad_k_t, 0).T * scale,
            jnp.concatenate(grad_v_t, 0).T,
        )
        for k, part in enumerate(parts):
            cols = pl.ds(pl.multiple_of(k * own + pair * step, step), step)
            part_low = part.astype(BF)
            out[:, cols] = part_low
            sums[:, cols] = jnp.sum(part_low.astype(F32), 0, keepdims=True)

    def two_pairs(k, carry):
        pair = 2 * k
        grad_probs(pair + 1, dp_b)
        grad_scores(pair, dp_a, ds_a)
        grad_probs(jnp.minimum(pair + 2, pairs - 1), dp_a)
        results(pair, ds_a)
        grad_scores(pair + 1, dp_b, ds_b)
        results(pair + 1, ds_b)
        return carry

    grad_probs(0, dp_a)
    lax.fori_loop(0, pairs // 2, two_pairs, 0)


def input_back_kernel(left, right, w_qkv, grad_first, out, work):
    width = out.shape[1]
    for k in range(3):
        at = k * width
        for part in (left, right):
            own = part.shape[1] // 3
            work[:, at : at + own] = part[:, k * own : (k + 1) * own]
            at += own
    block = 256
    for i in range(width // block):
        cols = slice(i * block, (i + 1) * block)
        value = grad_first[:, cols] + nt(work[...], w_qkv[cols, :])
        out[:, cols] = value.astype(BF)


def slot_device(me, order, slot):
    mixed = 0
    for j, b in enumerate(order):
        mixed = mixed | (((slot >> (len(order) - 1 - j)) & 1) << b)
    return me ^ mixed


def spread_shares(place, work, outs, order):
    me = place[1]
    if len(outs) == 1:
        outs = (outs[0].at[0], outs[0].at[1])
        me = me & ~(1 << order[0])
    keep, *sends = outs
    half, share, _ = keep.shape
    for slot in range(2 * half):
        ref, at = (keep, slot) if slot < half else piece_of(sends, slot - half)
        device = slot_device(me, order, slot)
        ref[at] = work[pl.ds(pl.multiple_of(device * share, 16), share), :]


def piece_of(refs, slot):
    size = refs[0].shape[0]
    return refs[slot // size], slot % size


def weight_grad_kernel(place, *refs, order, pairs):
    *outs, work = refs[2 * pairs :]
    block = 768

    def run(i):
        return pl.ds(pl.multiple_of(i * block, block), block)

    at = 0
    for left, right in zip(refs[: 2 * pairs : 2], refs[1 : 2 * pairs : 2]):
        rows, cols = left.shape[1], right.shape[1]

        def by_rows(i, carry, left=left, right=right, at=at, cols=cols):
            work[run(i), at : at + cols] = tn(left[:, run(i)], right[...]).astype(BF)
            return carry

        def by_columns(i, carry, left=left, right=right, at=at):
            there = pl.ds(pl.multiple_of(at + i * block, 128), block)
            work[:, there] = tn(left[...], right[:, run(i)]).astype(BF)
            return carry

        if rows > block:
            lax.fori_loop(0, rows // block, by_rows, 0)
        else:
            lax.fori_loop(0, cols // block, by_columns, 0)
        at += cols
    spread_shares(place, work, outs, order)


def last_grad_kernel(
    place, x, grad_proj, sums_two, sums_one, sums_left, sums_right, sums_in, *refs, order
):
    *outs, work = refs
    width = x.shape[1]
    share = outs[0].shape[1]
    devices = 2 * outs[0].shape[0]
    wide = grad_proj.shape[1]
    work[:, :wide] = tn(x[...], grad_proj[...]).astype(BF)
    extra = slice(wide, wide + 128)
    thirds = [sums.shape[1] // 3 for sums in (sums_left, sums_right)]
    query, value = (
        jnp.concatenate(
            [sums[:, k * own : (k + 1) * own] for sums, own in zip((sums_left, sums_right), thirds)], 1
        )
        for k in (0, 2)
    )
    stacked = jnp.concatenate([query, value, sums_two[0:3], sums_one[0:3]], 0)
    work[:, extra] = jnp.zeros((width, 128), BF)
    in_share = sums_in.shape[1] // devices
    for d in range(devices):
        rows = [stacked[:, d * share : (d + 1) * share]]
        for k in range(in_share // share):
            at = d * in_share + k * share
            rows.append(sums_in[:, at : at + share])
        rows.append(jnp.zeros((16 - 8 - in_share // share, share), F32))
        block = jnp.concatenate(rows, 0)
        block = jnp.concatenate([block, jnp.zeros((16, 128 - share), F32)], 1)
        high = block.astype(BF)
        work[d * share : d * share + 16, extra] = high
        work[d * share + 16 : d * share + 32, extra] = (block - high.astype(F32)).astype(BF)
    spread_shares(place, work, outs, order)


def add_extra(left, right):
    total = (
        left[0:16].astype(F32) + left[16:32].astype(F32) + right[0:16].astype(F32) + right[16:32].astype(F32)
    )
    return total


def halve_kernel(*refs, cames, extra):
    kept, came, (keep, *sends) = refs[0], refs[1 : 1 + cames], refs[1 + cames :]
    half = keep.shape[0]
    cols = keep.shape[2] - extra
    for slot in range(2 * half):
        ref, at = (keep, slot) if slot < half else piece_of(sends, slot - half)
        other, there = piece_of(came, slot)
        ref[at, :, :cols] = (kept[slot, :, :cols].astype(F32) + other[there, :, :cols].astype(F32)).astype(BF)
        if extra:
            total = add_extra(kept[slot, :, cols:], other[there, :, cols:])
            high = total.astype(BF)
            ref[at, 0:16, cols:] = high
            ref[at, 16:32, cols:] = (total - high.astype(F32)).astype(BF)
            ref[at, 32:, cols:] = jnp.zeros((keep.shape[1] - 32, extra), BF)


def halve_cores_kernel(both, *outs, extra):
    halve_kernel(both.at[0], both.at[1], *outs, cames=1, extra=extra)


def finish_kernel(kept, came, out):
    out[...] = kept[0].astype(F32) + came[0].astype(F32)


def finish_last_kernel(
    kept, came, kept_last, came_last, w_qkv, w_out, bq, bv, gain2, bias2, b_back, gain1, bias1, b_out, b_in
):
    width = w_out.shape[1]
    share = bq.shape[1]
    left, right = (kept.shape[2] - width) // 3, (kept_last.shape[2] - 128) // 3
    for k in range(3):
        at = k * width
        cols = slice(k * left, (k + 1) * left)
        w_qkv[:, at : at + left] = kept[0, :, cols].astype(F32) + came[0, :, cols].astype(F32)
        cols = slice(k * right, (k + 1) * right)
        w_qkv[:, at + left : at + width] = kept_last[0, :, cols].astype(F32) + came_last[0, :, cols].astype(F32)
    w_out[...] = kept[0, :, 3 * left :].astype(F32) + came[0, :, 3 * left :].astype(F32)
    vectors = add_extra(kept_last[0, :, 3 * right :], came_last[0, :, 3 * right :])
    for k, ref in enumerate((bq, bv, gain2, bias2, b_back, gain1, bias1, b_out)):
        ref[...] = vectors[k : k + 1, :share]
    pieces = b_in.shape[1] // share
    b_in[...] = jnp.concatenate([vectors[8 + k : 9 + k, :share] for k in range(pieces)], 1)


def plain_grad_kernel(left, right, out):
    out[...] = tn(left[...], right[...])


def swapped(value, axis, mask):
    count = lax.axis_size(axis)
    return lax.ppermute(value, axis, [(i, i ^ mask) for i in range(count)])


class Sequence:
    def __init__(self):
        self.last = None

    def now(self, value):
        return value if self.last is None else after(value, self.last)

    def ran(self, results):
        self.last = results[0]
        return results

    def chunk(self, outs, extra=0, pieces=1):
        chunk = {"extra": extra}
        if len(outs) > 1:
            chunk["keep"], *chunk["sends"] = self.ran(outs)
        else:
            pairs = [[i, i + 1] for i in range(0, lax.axis_size("dp"), 2)]
            both = lax.all_to_all(outs[0], "dp", 0, 0, tiled=True, axis_index_groups=pairs)
            self.last = both
            self.parted(chunk, functools.partial(halve_cores_kernel, extra=extra), [both], both.shape[1:], pieces)
        return chunk

    def parted(self, chunk, body, args, shape, pieces):
        half = sds((shape[0] // 2,) + shape[1:], BF)
        piece = sds((shape[0] // 2 // pieces,) + shape[1:], BF)
        chunk["keep"], *chunk["sends"] = self.ran(
            kernel_call(body, [half] + [piece] * pieces, args, mib=4, name="halve")
        )

    def go(self, chunk, bit, behind=None):
        sends = [self.now(send) for send in chunk["sends"]]
        if behind is not None:
            sends = [after(send, *behind["came"]) for send in sends]
        chunk["came"] = [swapped(send, "dp", 1 << bit) for send in sends]

    def take(self, chunk, pieces=1):
        keep, came = chunk["keep"], [self.now(value) for value in chunk["came"]]
        body = functools.partial(halve_kernel, cames=len(came), extra=chunk["extra"])
        self.parted(chunk, body, [keep] + came, keep.shape, pieces)

    def finish(self, chunk):
        args = [chunk["keep"], self.now(chunk["came"][0])]
        return self.ran([kernel_call(finish_kernel, sds(args[0].shape[1:], F32), args, mib=4, name="finish")])[0]


def after(value, *earlier):
    return lax.optimization_barrier((value,) + earlier)[0]


def shards(
    hidden_in,
    seg_ids,
    labels,
    out_grad,
    w_qkv,
    b_query,
    b_value,
    w_out,
    b_out,
    ln1_gain,
    ln1_bias,
    w_in,
    b_in,
    w_back,
    b_back,
    ln2_gain,
    ln2_bias,
):
    x, cotangent = hidden_in[0], out_grad[0]
    w_qkv, w_out, w_in, w_back = w_qkv[0], w_out[0], w_in[0], w_back[0]
    length, width = x.shape
    hidden = w_in.shape[1]
    heads = width // HEAD_DIM
    count = length // QLEN
    devices = lax.axis_size("dp")
    bits = devices.bit_length() - 1
    tower, me = lax.axis_index("tower"), lax.axis_index("dp")
    place = jnp.stack([tower, me]).astype(jnp.int32)
    seg_col = seg_ids.reshape(length, 1)
    fast = devices == 16

    proj = kernel_call(
        proj_kernel, sds((length, 3 * width), BF),
        [pltpu.with_memory_space_constraint(member, pltpu.HBM) for member in (x, w_qkv, b_query, b_value)], hbm=4,
        scratch=[pltpu.VMEM((length, width), BF)] + [pltpu.VMEM((width, width), BF)] * 3
        + [pltpu.VMEM((1, width), F32)] * 2 + [pltpu.SemaphoreType.DMA((6,))],
        mib=8, flops=2 * length * 3 * width * width, name="proj",
    )
    cls = kernel_call(
        cls_kernel, sds((count, width), BF),
        [place, seg_ids, x, proj, w_out, b_out, ln1_gain, ln1_bias, w_in, b_in, w_back, b_back,
         ln2_gain, ln2_bias],
        smem=1, mib=3, flops=2 * 256 * width * hidden * 2, name="cls",
    )
    other = swapped(cls, "tower", 1)
    attended, probs = kernel_call(
        attention_kernel, [sds((length, width), BF), sds((heads, length, length), BF)],
        [place, seg_ids, seg_col, after(proj, cls)], smem=1,
        scratch=[pltpu.VMEM((length, length), F32)] + [pltpu.VMEM((2, length, length), F32)] * 2,
        mib=9, flops=4 * heads * length * length * 256, name="attention",
    )
    held = kernel_call(
        packet_kernel, sds((PACKET, width), BF), [place, cls, after(other, attended), labels[None]],
        smem=1, mib=1, name="packet",
    )
    order = [3, 2, 1, 0] if fast else list(range(bits))
    if fast:
        came = swapped(held, "dp", 1 << order[0])
    work, half_work = pltpu.VMEM((length, width), F32), pltpu.VMEM((length // 2, width), F32)
    n1, r1, first_low = kernel_call(
        first_kernel,
        [sds((length, width), F32), sds((length, 1), F32), sds((length, width), BF)],
        [x, after(attended, held), w_out, b_out, ln1_gain, ln1_bias], scratch=[work],
        mib=4, flops=2 * length * width * width, name="first",
    )
    if fast:
        held = jnp.concatenate([held, after(came, first_low)], 0)
        came = swapped(held, "dp", 1 << order[1])
    act, slope = kernel_call(
        inner_kernel, [sds((length, hidden), BF), sds((length, hidden), BF)],
        [after(first_low, held), w_in, b_in], scratch=[pltpu.VMEM((length, 256), F32)] * 2,
        mib=4, flops=8 * length * width * hidden, name="inner",
    )
    if fast:
        held = jnp.concatenate([held, after(came, act)], 0)
        came = swapped(held, "dp", 1 << order[2])
    n2, r2, out_hidden = kernel_call(
        second_kernel,
        [sds((length, width), F32), sds((length, 1), F32), sds((length, width), BF)],
        [after(act, held), w_back, b_back, n1, ln1_gain, ln1_bias, ln2_gain, ln2_bias], scratch=[half_work],
        mib=5, flops=2 * length * width * hidden, name="second",
    )
    if fast:
        near = jnp.concatenate([held, after(came, out_hidden)], 0)
        far = swapped(near, "dp", 1 << order[3])
        cls_grad = kernel_call(
            functools.partial(loss_kernel, order=order, count=count), sds((count, width), F32),
            [place, near, far], smem=1,
            mib=5, flops=8 * devices * count * devices * SEGS * width, name="loss",
        )
    else:
        packets = lax.all_gather(held, "dp", axis=0)
        cls_grad = plain_loss(packets, tower, me, count)

    grad_second, second_low, sums_two = kernel_call(
        second_back_kernel,
        [sds((length, width), F32), sds((length, width), BF), sds((8, width), F32)],
        [place, seg_ids, cotangent, cls_grad, n2, r2, ln2_gain], smem=1, scratch=[work],
        mib=4, flops=2 * length * width * 256, name="second_back",
    )

    def plain_grad(left, right, name):
        rows, cols = left.shape[1], right.shape[1]
        whole = kernel_call(
            plain_grad_kernel, sds((rows, cols), F32), [left, right], mib=24,
            flops=2 * length * rows * cols, name=name,
        )
        return lax.psum_scatter(whole, "dp", scatter_dimension=0, tiled=True)

    inner_call = dict(mib=3, flops=2 * length * width * hidden, name="inner_back")
    inner_shape = [sds((length, hidden), BF), sds((1, hidden), F32)]
    first_call = dict(
        scratch=[half_work], mib=5, flops=2 * length * width * (hidden + width), name="first_back"
    )
    first_shape = [
        sds((length, width), F32), sds((length, width), BF), sds((length, width), BF), sds((8, width), F32)
    ]
    def attention_back(gradient, first, pairs):
        step = (length, length)
        return kernel_call(
            functools.partial(attention_back_kernel, first=first),
            [sds((length, 6 * HEAD_DIM * pairs), BF), sds((1, 6 * HEAD_DIM * pairs), F32)],
            [proj, probs, gradient],
            scratch=[pltpu.VMEM((2,) + step, F32)] * 2 + [pltpu.VMEM((2,) + step, BF)] * 2,
            mib=9, flops=16 * pairs * length * length * 256, name=f"attention_back_{first}",
        )

    head_pairs = heads // 2
    split = 2 * head_pairs // 3

    def input_back(left, right):
        return kernel_call(
            input_back_kernel, sds((length, width), BF), [left, right, w_qkv, grad_first],
            scratch=[pltpu.VMEM((length, 3 * width), BF)],
            mib=5, flops=6 * length * width * width, name="input_back",
        )

    if fast:
        share = width // devices
        line = Sequence()

        CORE, X, Z1, Z2 = range(4)

        def grads(*pairs, name, order=(CORE, X, Z1, Z2), pieces=1, at_once=False):
            rows = pairs[0][0].shape[1]
            shape = (devices // 2, rows // devices, sum(right.shape[1] for _, right in pairs))
            args = [member for left, right in pairs for member in (left, line.now(right))]
            outs = kernel_call(
                functools.partial(weight_grad_kernel, order=order, pairs=len(pairs)),
                [sds((2,) + shape, BF)] if at_once
                else [sds(shape, BF)] + [sds((shape[0] // pieces,) + shape[1:], BF)] * pieces,
                [place] + args, smem=1, scratch=[pltpu.VMEM((rows, shape[2]), BF)],
                mib=8, flops=2 * length * rows * shape[2], name=name,
            )
            return line.chunk(outs, pieces=pieces)

        a = grads((act, second_low), name="grad_w_back", order=(CORE, Z1, Z2, X))
        line.go(a, CORE)
        inner_low, sums_in = line.ran(
            kernel_call(inner_back_kernel, inner_shape, [line.now(second_low), w_back, slope], **inner_call)
        )
        line.take(a)
        line.go(a, Z1)
        b = grads((first_low, inner_low), name="grad_w_in", pieces=1)
        line.go(b, CORE)
        grad_first, branch_low, att_grad, sums_one = line.ran(
            kernel_call(
                first_back_kernel, first_shape,
                [line.now(inner_low), w_in, grad_second, n1, r1, ln1_gain, w_out], **first_call
            )
        )
        line.take(b)
        line.go(b, X)
        grad_left, sums_left = line.ran(attention_back(line.now(att_grad), 0, split))
        c = grads((x, grad_left), (attended, branch_low), name="grad_w_qkv_1", pieces=1)
        line.go(c, CORE)
        grad_right, sums_right = line.ran(attention_back(line.now(att_grad), split, head_pairs - split))
        line.take(c, pieces=2)
        line.take(a)
        line.go(a, Z2)
        cols = 6 * HEAD_DIM * (head_pairs - split) + 128
        d = line.chunk(
            kernel_call(
                functools.partial(last_grad_kernel, order=(CORE, X, Z1, Z2)),
                [sds((devices // 2, share, cols), BF)] + [sds((devices // 2 // 1, share, cols), BF)] * 1,
                [place, x, line.now(grad_right), sums_two, sums_one, sums_left, sums_right, sums_in],
                smem=1, scratch=[pltpu.VMEM((width, cols), BF)], mib=5,
                flops=2 * length * width * cols, name="grad_w_qkv_2",
            ),
            extra=128,
        )
        line.go(d, CORE)
        grad_hidden = line.ran([input_back(grad_left, line.now(grad_right))])[0]
        line.take(d)
        line.go(c, X, behind=b)
        line.take(b, pieces=2)
        line.go(b, Z1)
        line.take(a)
        line.go(d, X, behind=c)
        line.take(c, pieces=2)
        line.go(c, Z1)
        line.take(b)
        line.go(b, Z2)
        line.go(a, X, behind=d)
        line.take(d)
        line.go(d, Z1)
        line.take(c)
        line.go(c, Z2)
        share_w_in = line.finish(b)
        line.take(d)
        line.go(d, Z2)
        share_w_back = line.finish(a)
        (
            share_w_qkv, share_w_out, share_bq, share_bv, share_gain2, share_bias2, share_b_back,
            share_gain1, share_bias1, share_b_out, share_b_in,
        ) = kernel_call(
            finish_last_kernel,
            [sds((share, 3 * width), F32), sds((share, width), F32)] + [sds((1, share), F32)] * 8
            + [sds((1, hidden // devices), F32)],
            [c["keep"], line.now(c["came"][0]), d["keep"], d["came"][0]], mib=4, name="finish_last",
        )
    else:
        share_w_back = plain_grad(act, second_low, "grad_w_back")
        inner_low, sums_in = kernel_call(
            inner_back_kernel, inner_shape, [second_low, w_back, slope], **inner_call
        )
        share_w_in = plain_grad(first_low, inner_low, "grad_w_in")
        grad_first, branch_low, att_grad, sums_one = kernel_call(
            first_back_kernel, first_shape, [inner_low, w_in, grad_second, n1, r1, ln1_gain, w_out],
            **first_call
        )
        grad_left, sums_left = attention_back(att_grad, 0, split)
        grad_right, sums_right = attention_back(att_grad, split, head_pairs - split)
        grad_hidden = input_back(grad_left, grad_right)

        def joined(left, right):
            pieces = [jnp.split(half, 3, 1) for half in (left, right)]
            return jnp.concatenate([piece for both in zip(*pieces) for piece in both], 1)

        grad_proj, sums_qkv = joined(grad_left, grad_right), joined(sums_left, sums_right)
        share_w_qkv = plain_grad(x, grad_proj, "grad_w_qkv")
        share_w_out = plain_grad(attended, branch_low, "grad_w_out")

        def scattered(vector):
            return lax.psum_scatter(vector, "dp", scatter_dimension=1, tiled=True)

        share_bq, share_bv = scattered(sums_qkv[:, :width]), scattered(sums_qkv[:, 2 * width :])
        share_gain2, share_bias2, share_b_back = (scattered(sums_two[k : k + 1]) for k in range(3))
        share_gain1, share_bias1, share_b_out = (scattered(sums_one[k : k + 1]) for k in range(3))
        share_b_in = scattered(sums_in)
    return (
        out_hidden[None],
        grad_hidden[None],
        share_w_qkv[None],
        share_bq,
        share_bv,
        share_w_out[None],
        share_b_out,
        share_gain1,
        share_bias1,
        share_w_in[None],
        share_b_in,
        share_w_back[None],
        share_b_back,
        share_gain2,
        share_bias2,
    )


def solution(mesh):
    matrix, vector = P("tower", None, None), P("tower", None)
    rows, spread = P("tower", "dp", None), P("tower", "dp")
    return jax.shard_map(
        shards,
        mesh=mesh,
        in_specs=(
            rows, P("dp", None), P("dp"), rows, matrix, vector, vector, matrix, vector, vector, vector,
            matrix, vector, matrix, vector, vector, vector,
        ),
        out_specs=(
            rows, rows, rows, spread, spread, rows, spread, spread, spread, rows, spread, rows, spread,
            spread, spread,
        ),
        check_vma=False,
    )
```

profile of v0, /device:TPU:0, one launch (start us, length us, event | category | flops | bytes accessed | tf_op | source)
XLA Modules:
  0.0 161.5 jit_solution(15599573745553479594)
XLA Ops:
  0.8 4.7 %proj.1 = bf16[512,2304]{1,0:T(8,128)(2,1)S(1)} custom-call(bf16[512,768]{1,0:T(8,128)(2,1)} %bitcast.19, bf16[768,2304]{1,0:T(8,128)(2,1)} %bitcast.32, f32[1,768]{1,0:T(1,128)} %bq_hbm.1, f32[1,768]{1,0:T(1,128)} %bv_hbm.1), custom_call_target="tpu_custom_call" | custom-call | tf_op jit(solution)/shard_map/proj/pallas_call | solution.py:42
  5.5 2.3 %copy-done.3 = bf16[1,768,3072]{2,1,0:T(8,128)(2,1)S(1)} copy-done((bf16[1,768,3072]{2,1,0:T(8,128)(2,1)S(1)}, bf16[1,768,3072]{2,1,0:T(8,128)(2,1)}, u32[]{:S(2)}) %copy-start.3) | copy-done | bytes 4718616
  10.6 3.8 %cls.1 = bf16[16,768]{1,0:T(8,128)(2,1)S(1)} custom-call(s32[2]{0:T(128)S(1)} %pad_add_fusion.place, s32[1,512]{1,0:T(1,128)S(1)} %copy-done.11, bf16[512,768]{1,0:T(8,128)(2,1)S(1)} %bitcast.20, bf16[512,2304]{1,0:T(8,128)(2,1)S(1)} %proj.1, bf16[768,768]{1,0:T(8,128)(2,1)S(1)} %bitcast.29, f32[1,768]{1,0:T(1,128)S(1)} %copy-done.15, ...), custom_call_target="tpu_custom_call" | custom-call | tf_op jit(solution)/shard_map/cls/pallas_call | solution.py:42
  14.4 3.0 %collective-permute-start = (bf16[16,768]{1,0:T(8,128)(2,1)S(1)}, bf16[16,768]{1,0:T(8,128)(2,1)S(1)}, u32[]{:S(2)}, u32[]{:S(2)}) collective-permute-start(bf16[16,768]{1,0:T(8,128)(2,1)S(1)} %cls.1), channel_id=1, source_target_pairs={{0,16},{16,0},{1,17},{17,1},{2,18},{18,2},{3,19},{19,3},{4,20},{20... | collective-permute-start | bytes 73736 | tf_op jit(solution)/shard_map/ppermute | solution.py:623
  17.6 7.0 %attention.1 = (bf16[512,768]{1,0:T(8,128)(2,1)S(1)}, bf16[12,512,512]{2,1,0:T(8,128)(2,1)S(1)}) custom-call(s32[2]{0:T(128)S(1)} %pad_add_fusion.place, s32[1,512]{1,0:T(1,128)S(1)} %copy-done.11, s32[512,1]{1,0:T(8,128)S(1)} %copy.32.seg_col, bf16[512,2304]{1,0:T(8,128)(2,1)S(1)} %proj.1), custom_call_target="tpu_custom_call" | custom-call | tf_op jit(solution)/shard_map/attention/pallas_call | solution.py:42
  25.2 2.7 %collective-permute-start.1 = (bf16[24,768]{1,0:T(8,128)(2,1)S(1)}, bf16[24,768]{1,0:T(8,128)(2,1)S(1)}, u32[]{:S(2)}, u32[]{:S(2)}) collective-permute-start(bf16[24,768]{1,0:T(8,128)(2,1)S(1)} %packet.1), channel_id=1, source_target_pairs={{0,8},{1,9},{2,10},{3,11},{4,12},{5,13},{6,14},{7,15},{8,0},{9,1},... | collective-permute-start | bytes 110600 | tf_op jit(solution)/shard_map/ppermute | solution.py:623
  27.9 1.7 %first.1 = (f32[512,768]{1,0:T(8,128)S(1)}, f32[512,1]{1,0:T(8,128)S(1)}, bf16[512,768]{1,0:T(8,128)(2,1)S(1)}) custom-call(bf16[512,768]{1,0:T(8,128)(2,1)S(1)} %bitcast.21, bf16[512,768]{1,0:T(8,128)(2,1)S(1)} %get-tuple-element.145.attended.refs_2_, bf16[768,768]{1,0:T(8,128)(2,1)S(1)} %bitcast.30, f32[1,768]{1,0:T(1,128)S(1)} %copy-done.16, ...), custom_call_target="tpu_custom_call" | custom-call | tf_op jit(solution)/shard_map/first/pallas_call | solution.py:42
  30.2 1.6 %collective-permute-start.2 = (bf16[48,768]{1,0:T(8,128)(2,1)S(1)}, bf16[48,768]{1,0:T(8,128)(2,1)S(1)}, u32[]{:S(2)}, u32[]{:S(2)}) collective-permute-start(bf16[48,768]{1,0:T(8,128)(2,1)S(1)} %pad_maximum_fusion.2), channel_id=1, source_target_pairs={{0,4},{1,5},{2,6},{3,7},{4,0},{5,1},{6,2},{7,3},{8,12},{9,13},{10,... | collective-permute-start | bytes 221192 | tf_op jit(solution)/shard_map/ppermute | solution.py:623
  31.8 2.3 %copy-done.4 = bf16[1,768,3072]{2,1,0:T(8,128)(2,1)S(1)} copy-done((bf16[1,768,3072]{2,1,0:T(8,128)(2,1)S(1)}, bf16[1,768,3072]{2,1,0:T(8,128)(2,1)}, u32[]{:S(2)}) %copy-start.4) | copy-done | bytes 4718616
  34.2 6.0 %inner.1 = (bf16[512,3072]{1,0:T(8,128)(2,1)S(1)}, bf16[512,3072]{1,0:T(8,128)(2,1)S(1)}) custom-call(bf16[512,768]{1,0:T(8,128)(2,1)S(1)} %get-tuple-element.148.low.refs_0_, bf16[768,3072]{1,0:T(8,128)(2,1)S(1)} %bitcast.25, f32[1,3072]{1,0:T(1,128)S(1)} %copy-done.10), custom_call_target="tpu_custom_call" | custom-call | tf_op jit(solution)/shard_map/inner/pallas_call | solution.py:42
  40.2 1.6 collective-permute-start.3
  41.7 4.2 %second.1 = (f32[512,768]{1,0:T(8,128)S(1)}, f32[512,1]{1,0:T(8,128)S(1)}, bf16[512,768]{1,0:T(8,128)(2,1)}) custom-call(bf16[512,3072]{1,0:T(8,128)(2,1)S(1)} %get-tuple-element.151.act.refs_0_, bf16[3072,768]{1,0:T(8,128)(2,1)S(1)} %bitcast.17, f32[1,768]{1,0:T(1,128)S(1)} %copy-done.18, f32[512,768]{1,0:T(8,128)S(1)} %get-tuple-element.152.n1, ...), custom_call_target="tpu_custom_call" | custom-call | tf_op jit(solution)/shard_map/second/pallas_call | solution.py:42
  46.0 1.6 collective-permute-done.4.far
  47.6 3.3 %loss.1.cls_grad = f32[16,768]{1,0:T(8,128)S(1)} custom-call(s32[2]{0:T(128)S(1)} %pad_add_fusion.place, bf16[192,768]{1,0:T(8,128)(2,1)S(1)} %pad_maximum_fusion.near, bf16[192,768]{1,0:T(8,128)(2,1)S(1)} %collective-permute-done.4.far), custom_call_target="tpu_custom_call" | custom-call | tf_op jit(solution)/shard_map/loss/pallas_call | solution.py:42
  50.9 1.9 %second_back.1 = (f32[512,768]{1,0:T(8,128)S(1)}, bf16[512,768]{1,0:T(8,128)(2,1)S(1)}, f32[8,768]{1,0:T(8,128)S(1)}) custom-call(s32[2]{0:T(128)S(1)} %pad_add_fusion.place, s32[1,512]{1,0:T(1,128)S(1)} %copy-done.11, bf16[512,768]{1,0:T(8,128)(2,1)S(1)} %bitcast.34, f32[16,768]{1,0:T(8,128)S(1)} %loss.1.cls_grad, f32[512,768]{1,0:T(8,128)S(1)} %get-tuple-element.156.n2, ...), custom_call_target="tpu_custom_call" | custom-call | tf_op jit(solution)/shard_map/second_back/pallas_call | solution.py:42
  52.8 4.3 %grad_w_back.1 = (bf16[8,192,768]{2,1,0:T(8,128)(2,1)S(1)}, bf16[8,192,768]{2,1,0:T(8,128)(2,1)S(1)}) custom-call(s32[2]{0:T(128)S(1)} %pad_add_fusion.place, bf16[512,3072]{1,0:T(8,128)(2,1)S(1)} %get-tuple-element.151.act.refs_0_, bf16[512,768]{1,0:T(8,128)(2,1)S(1)} %get-tuple-element.160.refs_1_.low), custom_call_target="tpu_custom_call" | custom-call | tf_op jit(solution)/shard_map/grad_w_back/pallas_call | solution.py:42
  57.3 4.1 %inner_back.1 = (bf16[512,3072]{1,0:T(8,128)(2,1)S(1)}, f32[1,3072]{1,0:T(1,128)S(1)}) custom-call(bf16[512,768]{1,0:T(8,128)(2,1)S(1)} %get-tuple-element.160.refs_1_.low, bf16[3072,768]{1,0:T(8,128)(2,1)S(1)} %bitcast.18, bf16[512,3072]{1,0:T(8,128)(2,1)S(1)} %get-tuple-element.161.slope), custom_call_target="tpu_custom_call" | custom-call | tf_op jit(solution)/shard_map/inner_back/pallas_call | solution.py:42
  63.0 4.4 %grad_w_in.1 = (bf16[8,48,3072]{2,1,0:T(8,128)(2,1)S(1)}, bf16[8,48,3072]{2,1,0:T(8,128)(2,1)S(1)}) custom-call(s32[2]{0:T(128)S(1)} %pad_add_fusion.place, bf16[512,768]{1,0:T(8,128)(2,1)S(1)} %get-tuple-element.148.low.refs_0_, bf16[512,3072]{1,0:T(8,128)(2,1)S(1)} %get-tuple-element.169.refs_1_.inner), custom_call_target="tpu_custom_call" | custom-call | tf_op jit(solution)/shard_map/grad_w_in/pallas_call | solution.py:42
  67.5 5.6 %first_back.1 = (f32[512,768]{1,0:T(8,128)S(1)}, bf16[512,768]{1,0:T(8,128)(2,1)S(1)}, bf16[512,768]{1,0:T(8,128)(2,1)S(1)}, f32[8,768]{1,0:T(8,128)S(1)}) custom-call(bf16[512,3072]{1,0:T(8,128)(2,1)S(1)} %get-tuple-element.169.refs_1_.inner, bf16[768,3072]{1,0:T(8,128)(2,1)S(1)} %bitcast.28, f32[512,768]{1,0:T(8,128)S(1)} %get-tuple-element.170.grad_second, ...), custom_call_target="tpu_custom_call" | custom-call | flops 30000001024 | tf_op jit(solution)/shard_map/first_back/pallas_call | solution.py:42
  73.7 1.0 collective-permute-start.10
  74.7 5.5 %attention_back_0.1 = (bf16[512,1536]{1,0:T(8,128)(2,1)S(1)}, f32[1,1536]{1,0:T(1,128)S(1)}) custom-call(bf16[512,2304]{1,0:T(8,128)(2,1)S(1)} %proj.1, bf16[12,512,512]{2,1,0:T(8,128)(2,1)S(1)} %get-tuple-element.154.probs, bf16[512,768]{1,0:T(8,128)(2,1)S(1)} %get-tuple-element.184.att_grad), custom_call_target="tpu_custom_call" | custom-call | tf_op jit(solution)/shard_map/attention_back_0/pallas_call | solution.py:42
  80.2 3.5 %grad_w_qkv_1.1 = (bf16[8,48,2304]{2,1,0:T(8,128)(2,1)S(1)}, bf16[8,48,2304]{2,1,0:T(8,128)(2,1)S(1)}) custom-call(s32[2]{0:T(128)S(1)} %pad_add_fusion.place, bf16[512,768]{1,0:T(8,128)(2,1)S(1)} %bitcast.22, bf16[512,1536]{1,0:T(8,128)(2,1)S(1)} %get-tuple-element.180.refs_1_.left, bf16[512,768]{1,0:T(8,128)(2,1)S(1)} %get-tuple-element.145.attended.refs_2_, ...), custom_call_target="tpu_custom_call" | custom-call | tf_op jit(solution)/shard_map/grad_w_qkv_1/pallas_call | solution.py:42
  84.0 2.7 %attention_back_4.1 = (bf16[512,768]{1,0:T(8,128)(2,1)S(1)}, f32[1,768]{1,0:T(1,128)S(1)}) custom-call(bf16[512,2304]{1,0:T(8,128)(2,1)S(1)} %proj.1, bf16[12,512,512]{2,1,0:T(8,128)(2,1)S(1)} %get-tuple-element.154.probs, bf16[512,768]{1,0:T(8,128)(2,1)S(1)} %get-tuple-element.184.att_grad), custom_call_target="tpu_custom_call" | custom-call | flops 30000001024 | tf_op jit(solution)/shard_map/attention_back_4/pallas_call | solution.py:42
  86.7 0.8 collective-permute-done.8.refs_1_
  87.9 2.4 %collective-permute-done.7.refs_1_ = bf16[4,192,768]{2,1,0:T(8,128)(2,1)S(1)} collective-permute-done((bf16[4,192,768]{2,1,0:T(8,128)(2,1)S(1)}, bf16[4,192,768]{2,1,0:T(8,128)(2,1)S(1)}, u32[]{:S(2)}, u32[]{:S(2)}) %collective-permute-start.7) | collective-permute-done | bytes 1179680 | tf_op jit(solution)/shard_map/ppermute | solution.py:623
  90.6 2.9 %collective-permute-start.12 = (bf16[2,192,768]{2,1,0:T(8,128)(2,1)S(1)}, bf16[2,192,768]{2,1,0:T(8,128)(2,1)S(1)}, u32[]{:S(2)}, u32[]{:S(2)}) collective-permute-start(bf16[2,192,768]{2,1,0:T(8,128)(2,1)S(1)} %get-tuple-element.212), channel_id=1, source_target_pairs={{0,8},{1,9},{2,10},{3,11},{4,12},{5,13},{6,14},{7,15},{8,0},{9,1},... | collective-permute-start | bytes 1769480 | tf_op jit(solution)/shard_map/ppermute | solution.py:623
  93.5 1.5 grad_w_qkv_2.1
  95.1 2.9 %input_back.1 = bf16[512,768]{1,0:T(8,128)(2,1)} custom-call(bf16[512,1536]{1,0:T(8,128)(2,1)S(1)} %get-tuple-element.180.refs_1_.left, bf16[512,768]{1,0:T(8,128)(2,1)S(1)} %get-tuple-element.201.grad_proj.right, bf16[768,2304]{1,0:T(8,128)(2,1)S(1)} %bitcast.33, f32[512,768]{1,0:T(8,128)S(1)} %get-tuple-element.175.grad_first), custom_call_target="tpu_custom_call" | custom-call | flops 30000001024 | tf_op jit(solution)/shard_map/input_back/pallas_call | solution.py:42
  98.2 3.9 %collective-permute-done.10.refs_1_ = bf16[4,48,3072]{2,1,0:T(8,128)(2,1)S(1)} collective-permute-done((bf16[4,48,3072]{2,1,0:T(8,128)(2,1)S(1)}, bf16[4,48,3072]{2,1,0:T(8,128)(2,1)S(1)}, u32[]{:S(2)}, u32[]{:S(2)}) %collective-permute-start.10) | collective-permute-done | bytes 1179680 | tf_op jit(solution)/shard_map/ppermute | solution.py:623
  102.1 0.9 collective-permute-start.11
  103.0 1.1 collective-permute-start.13
  104.4 1.4 collective-permute-start.17
  106.4 12.5 %collective-permute-done.12.refs_1_ = bf16[2,192,768]{2,1,0:T(8,128)(2,1)S(1)} collective-permute-done((bf16[2,192,768]{2,1,0:T(8,128)(2,1)S(1)}, bf16[2,192,768]{2,1,0:T(8,128)(2,1)S(1)}, u32[]{:S(2)}, u32[]{:S(2)}) %collective-permute-start.12) | collective-permute-done | bytes 589856 | tf_op jit(solution)/shard_map/ppermute | solution.py:623
  119.1 4.2 %collective-permute-done.13.refs_2_ = bf16[2,48,2304]{2,1,0:T(8,128)(2,1)S(1)} collective-permute-done((bf16[2,48,2304]{2,1,0:T(8,128)(2,1)S(1)}, bf16[2,48,2304]{2,1,0:T(8,128)(2,1)S(1)}, u32[]{:S(2)}, u32[]{:S(2)}) %collective-permute-start.13) | collective-permute-done | bytes 442400 | tf_op jit(solution)/shard_map/ppermute | solution.py:623
  123.3 0.9 collective-permute-start.15
  124.4 1.4 collective-permute-start.18
  126.5 5.1 %collective-permute-done.16.refs_1_ = bf16[1,48,3072]{2,1,0:T(8,128)(2,1)S(1)} collective-permute-done((bf16[1,48,3072]{2,1,0:T(8,128)(2,1)S(1)}, bf16[1,48,3072]{2,1,0:T(8,128)(2,1)S(1)}, u32[]{:S(2)}, u32[]{:S(2)}) %collective-permute-start.16) | collective-permute-done | bytes 294944 | tf_op jit(solution)/shard_map/ppermute | solution.py:623
  132.5 0.9 collective-permute-start.20
  133.5 2.5 %collective-permute-start.21 = (bf16[2,48,896]{2,1,0:T(8,128)(2,1)S(1)}, bf16[2,48,896]{2,1,0:T(8,128)(2,1)S(1)}, u32[]{:S(2)}, u32[]{:S(2)}) collective-permute-start(bf16[2,48,896]{2,1,0:T(8,128)(2,1)S(1)} %get-tuple-element.248), channel_id=1, source_target_pairs={{0,4},{1,5},{2,6},{3,7},{4,0},{5,1},{6,2},{7,3},{8,12},{9,13},{10,... | collective-permute-start | bytes 516104 | tf_op jit(solution)/shard_map/ppermute | solution.py:623
  136.1 1.8 %collective-permute-done.18.refs_2_ = bf16[1,48,2304]{2,1,0:T(8,128)(2,1)S(1)} collective-permute-done((bf16[1,48,2304]{2,1,0:T(8,128)(2,1)S(1)}, bf16[1,48,2304]{2,1,0:T(8,128)(2,1)S(1)}, u32[]{:S(2)}, u32[]{:S(2)}) %collective-permute-start.18) | collective-permute-done | bytes 221216 | tf_op jit(solution)/shard_map/ppermute | solution.py:623
  137.9 7.5 %collective-permute-done.14.refs_1_ = bf16[1,48,2304]{2,1,0:T(8,128)(2,1)S(1)} collective-permute-done((bf16[1,48,2304]{2,1,0:T(8,128)(2,1)S(1)}, bf16[1,48,2304]{2,1,0:T(8,128)(2,1)S(1)}, u32[]{:S(2)}, u32[]{:S(2)}) %collective-permute-start.14) | collective-permute-done | bytes 221216 | tf_op jit(solution)/shard_map/ppermute | solution.py:623
  145.5 2.6 %collective-permute-start.19 = (bf16[1,48,2304]{2,1,0:T(8,128)(2,1)S(1)}, bf16[1,48,2304]{2,1,0:T(8,128)(2,1)S(1)}, u32[]{:S(2)}, u32[]{:S(2)}) collective-permute-start(bf16[1,48,2304]{2,1,0:T(8,128)(2,1)S(1)} %get-tuple-element.243), channel_id=1, source_target_pairs={{0,8},{1,9},{2,10},{3,11},{4,12},{5,13},{6,14},{7,15},{8,0},{9,1},... | collective-permute-start | bytes 663560 | tf_op jit(solution)/shard_map/ppermute | solution.py:623
  148.1 0.9 finish.2
  149.0 3.8 %collective-permute-done.21.refs_1_ = bf16[2,48,896]{2,1,0:T(8,128)(2,1)S(1)} collective-permute-done((bf16[2,48,896]{2,1,0:T(8,128)(2,1)S(1)}, bf16[2,48,896]{2,1,0:T(8,128)(2,1)S(1)}, u32[]{:S(2)}, u32[]{:S(2)}) %collective-permute-start.21) | collective-permute-done | bytes 172064 | tf_op jit(solution)/shard_map/ppermute | solution.py:623
  152.9 0.9 finish.3
  153.8 5.2 %collective-permute-done.19.came = bf16[1,48,2304]{2,1,0:T(8,128)(2,1)S(1)} collective-permute-done((bf16[1,48,2304]{2,1,0:T(8,128)(2,1)S(1)}, bf16[1,48,2304]{2,1,0:T(8,128)(2,1)S(1)}, u32[]{:S(2)}, u32[]{:S(2)}) %collective-permute-start.19) | collective-permute-done | bytes 221216 | tf_op jit(solution)/shard_map/ppermute | solution.py:623
  159.0 1.6 %collective-permute-done.23.came_last = bf16[1,48,896]{2,1,0:T(8,128)(2,1)S(1)} collective-permute-done((bf16[1,48,896]{2,1,0:T(8,128)(2,1)S(1)}, bf16[1,48,896]{2,1,0:T(8,128)(2,1)S(1)}, u32[]{:S(2)}, u32[]{:S(2)}) %collective-permute-start.23) | collective-permute-done | bytes 86048 | tf_op jit(solution)/shard_map/ppermute | solution.py:623
  160.6 0.9 finish_last.1
  (87 shorter events, 11.0 us)
Async XLA Ops:
  0.7 4.7 %copy-start = (bf16[1,3072,768]{2,1,0:T(8,128)(2,1)S(1)}, bf16[1,3072,768]{2,1,0:T(8,128)(2,1)}, u32[]{:S(2)}) copy-start(bf16[1,3072,768]{2,1,0:T(8,128)(2,1)} %param.30) | copy-start | bytes 14155780
  0.7 4.7 %copy-start.2 = (bf16[1,512,768]{2,1,0:T(8,128)(2,1)S(1)}, bf16[1,512,768]{2,1,0:T(8,128)(2,1)}, u32[]{:S(2)}) copy-start(bf16[1,512,768]{2,1,0:T(8,128)(2,1)} %param.17) | copy-start | bytes 2359300
  0.7 4.7 %copy-start.5 = (bf16[1,768,768]{2,1,0:T(8,128)(2,1)S(1)}, bf16[1,768,768]{2,1,0:T(8,128)(2,1)}, u32[]{:S(2)}) copy-start(bf16[1,768,768]{2,1,0:T(8,128)(2,1)} %param.24) | copy-start | bytes 3538948
  0.7 4.8 %copy-start.11 = (s32[1,512]{1,0:T(1,128)S(1)}, s32[1,512]{1,0:T(1,128)}, u32[]{:S(2)}) copy-start(s32[1,512]{1,0:T(1,128)} %seg.3) | copy-start | bytes 6148
  0.7 4.8 %copy-start.12 = (f32[1,768]{1,0:T(1,128)S(1)}, f32[1,768]{1,0:T(1,128)}, u32[]{:S(2)}) copy-start(f32[1,768]{1,0:T(1,128)} %b1.5) | copy-start | bytes 9220
  0.7 4.8 %copy-start.13 = (f32[1,768]{1,0:T(1,128)S(1)}, f32[1,768]{1,0:T(1,128)}, u32[]{:S(2)}) copy-start(f32[1,768]{1,0:T(1,128)} %g1.7) | copy-start | bytes 9220
  0.8 4.8 %copy-start.14 = (f32[1,768]{1,0:T(1,128)S(1)}, f32[1,768]{1,0:T(1,128)}, u32[]{:S(2)}) copy-start(f32[1,768]{1,0:T(1,128)} %g2.5) | copy-start | bytes 9220
  5.5 2.3 %copy-start.3 = (bf16[1,768,3072]{2,1,0:T(8,128)(2,1)S(1)}, bf16[1,768,3072]{2,1,0:T(8,128)(2,1)}, u32[]{:S(2)}) copy-start(bf16[1,768,3072]{2,1,0:T(8,128)(2,1)} %param.28) | copy-start | bytes 14155780
  7.9 0.7 copy-start.9
  8.6 0.7 copy-start.15
  9.3 0.7 copy-start.17
  9.9 0.7 copy-start.19
  14.4 10.3 %copy-start.21 = (s32[16]{0:T(128)S(1)}, s32[16]{0:T(128)}, u32[]{:S(2)}) copy-start(s32[16]{0:T(128)} %param.19) | copy-start | bytes 196
  14.4 13.5 %copy-start.16 = (f32[1,768]{1,0:T(1,128)S(1)}, f32[1,768]{1,0:T(1,128)}, u32[]{:S(2)}) copy-start(f32[1,768]{1,0:T(1,128)} %b_out.3) | copy-start | bytes 9220
  14.4 10.2 %collective-permute-start = (bf16[16,768]{1,0:T(8,128)(2,1)S(1)}, bf16[16,768]{1,0:T(8,128)(2,1)S(1)}, u32[]{:S(2)}, u32[]{:S(2)}) collective-permute-start(bf16[16,768]{1,0:T(8,128)(2,1)S(1)} %cls.1), channel_id=1, source_target_pairs={{0,16},{16,0},{1,17},{17,1},{2,18},{18,2},{3,19},{19,3},{4,20},{20... | collective-permute-start | bytes 73736 | tf_op jit(solution)/shard_map/ppermute | solution.py:623
  17.6 10.3 %copy-start.6 = (bf16[1,768,768]{2,1,0:T(8,128)(2,1)S(1)}, bf16[1,768,768]{2,1,0:T(8,128)(2,1)}, u32[]{:S(2)}) copy-start(bf16[1,768,768]{2,1,0:T(8,128)(2,1)} %param.24) | copy-start | bytes 3538948
  24.6 7.2 %copy-start.10 = (f32[1,3072]{1,0:T(1,128)S(1)}, f32[1,3072]{1,0:T(1,128)}, u32[]{:S(2)}) copy-start(f32[1,3072]{1,0:T(1,128)} %b_in.3) | copy-start | bytes 36868
  25.2 4.9 %collective-permute-start.1 = (bf16[24,768]{1,0:T(8,128)(2,1)S(1)}, bf16[24,768]{1,0:T(8,128)(2,1)S(1)}, u32[]{:S(2)}, u32[]{:S(2)}) collective-permute-start(bf16[24,768]{1,0:T(8,128)(2,1)S(1)} %packet.1), channel_id=1, source_target_pairs={{0,8},{1,9},{2,10},{3,11},{4,12},{5,13},{6,14},{7,15},{8,0},{9,1},... | collective-permute-start | bytes 110600 | tf_op jit(solution)/shard_map/ppermute | solution.py:623
  30.2 11.5 %copy-start.1 = (bf16[1,3072,768]{2,1,0:T(8,128)(2,1)S(1)}, bf16[1,3072,768]{2,1,0:T(8,128)(2,1)}, u32[]{:S(2)}) copy-start(bf16[1,3072,768]{2,1,0:T(8,128)(2,1)} %param.30) | copy-start | bytes 14155780
  30.2 10.0 %collective-permute-start.2 = (bf16[48,768]{1,0:T(8,128)(2,1)S(1)}, bf16[48,768]{1,0:T(8,128)(2,1)S(1)}, u32[]{:S(2)}, u32[]{:S(2)}) collective-permute-start(bf16[48,768]{1,0:T(8,128)(2,1)S(1)} %pad_maximum_fusion.2), channel_id=1, source_target_pairs={{0,4},{1,5},{2,6},{3,7},{4,0},{5,1},{6,2},{7,3},{8,12},{9,13},{10,... | collective-permute-start | bytes 221192 | tf_op jit(solution)/shard_map/ppermute | solution.py:623
  31.8 2.3 %copy-start.4 = (bf16[1,768,3072]{2,1,0:T(8,128)(2,1)S(1)}, bf16[1,768,3072]{2,1,0:T(8,128)(2,1)}, u32[]{:S(2)}) copy-start(bf16[1,768,3072]{2,1,0:T(8,128)(2,1)} %param.28) | copy-start | bytes 14155780
  34.2 7.6 %copy-start.18 = (f32[1,768]{1,0:T(1,128)S(1)}, f32[1,768]{1,0:T(1,128)}, u32[]{:S(2)}) copy-start(f32[1,768]{1,0:T(1,128)} %b_back.3) | copy-start | bytes 9220
  34.2 7.6 %copy-start.20 = (f32[1,768]{1,0:T(1,128)S(1)}, f32[1,768]{1,0:T(1,128)}, u32[]{:S(2)}) copy-start(f32[1,768]{1,0:T(1,128)} %b2.3) | copy-start | bytes 9220
  40.2 5.8 %collective-permute-start.3 = (bf16[96,768]{1,0:T(8,128)(2,1)S(1)}, bf16[96,768]{1,0:T(8,128)(2,1)S(1)}, u32[]{:S(2)}, u32[]{:S(2)}) collective-permute-start(bf16[96,768]{1,0:T(8,128)(2,1)S(1)} %pad_maximum_fusion.1), channel_id=1, source_target_pairs={{0,2},{1,3},{2,0},{3,1},{4,6},{5,7},{6,4},{7,5},{8,10},{9,11},{10,... | collective-permute-start | bytes 442376 | tf_op jit(solution)/shard_map/ppermute | solution.py:623
  45.9 4.9 %copy-start.8 = (bf16[1,512,768]{2,1,0:T(8,128)(2,1)S(1)}, bf16[1,512,768]{2,1,0:T(8,128)(2,1)}, u32[]{:S(2)}) copy-start(bf16[1,512,768]{2,1,0:T(8,128)(2,1)} %param.20) | copy-start | bytes 2359300
  45.9 1.6 %collective-permute-start.4 = (bf16[192,768]{1,0:T(8,128)(2,1)S(1)}, bf16[192,768]{1,0:T(8,128)(2,1)S(1)}, u32[]{:S(2)}, u32[]{:S(2)}) collective-permute-start(bf16[192,768]{1,0:T(8,128)(2,1)S(1)} %pad_maximum_fusion.near), channel_id=1, source_target_pairs={{0,1},{1,0},{2,3},{3,2},{4,5},{5,4},{6,7},{7,6},{8,9},{9,8},{10,11... | collective-permute-start | bytes 884744 | tf_op jit(solution)/shard_map/ppermute | solution.py:623
  57.1 4.6 %collective-permute-start.5 = (bf16[8,192,768]{2,1,0:T(8,128)(2,1)S(1)}, bf16[8,192,768]{2,1,0:T(8,128)(2,1)S(1)}, u32[]{:S(2)}, u32[]{:S(2)}) collective-permute-start(bf16[8,192,768]{2,1,0:T(8,128)(2,1)S(1)} %get-tuple-element.164), channel_id=1, source_target_pairs={{0,1},{1,0},{2,3},{3,2},{4,5},{5,4},{6,7},{7,6},{8,9},{9,8},{10,11... | collective-permute-start | bytes 7077896 | tf_op jit(solution)/shard_map/ppermute | solution.py:623
  57.3 10.2 %slice-start = ((s8[4718592]{0:T(1024)(128)(4,1)}), s8[524288]{0:T(1024)(128)(4,1)S(1)}, s32[]{:S(2)}) async-start(s8[4718592]{0:T(1024)(128)(4,1)} %bitcast.26), calls=%async_computation | async-start | bytes 1048576
  61.7 5.8 %slice-start.1 = ((s8[4718592]{0:T(1024)(128)(4,1)}), s8[4194304]{0:T(1024)(128)(4,1)S(1)}, s32[]{:S(2)}) async-start(s8[4718592]{0:T(1024)(128)(4,1)} %bitcast.26), calls=%async_computation.1 | async-start | bytes 8388608
  62.2 28.1 %collective-permute-start.7 = (bf16[4,192,768]{2,1,0:T(8,128)(2,1)S(1)}, bf16[4,192,768]{2,1,0:T(8,128)(2,1)S(1)}, u32[]{:S(2)}, u32[]{:S(2)}) collective-permute-start(bf16[4,192,768]{2,1,0:T(8,128)(2,1)S(1)} %get-tuple-element.187), channel_id=1, source_target_pairs={{0,4},{1,5},{2,6},{3,7},{4,0},{5,1},{6,2},{7,3},{8,12},{9,13},{10,... | collective-permute-start | bytes 3538952 | tf_op jit(solution)/shard_map/ppermute | solution.py:623
  67.4 5.7 %collective-permute-start.6 = (bf16[8,48,3072]{2,1,0:T(8,128)(2,1)S(1)}, bf16[8,48,3072]{2,1,0:T(8,128)(2,1)S(1)}, u32[]{:S(2)}, u32[]{:S(2)}) collective-permute-start(bf16[8,48,3072]{2,1,0:T(8,128)(2,1)S(1)} %get-tuple-element.174), channel_id=1, source_target_pairs={{0,1},{1,0},{2,3},{3,2},{4,5},{5,4},{6,7},{7,6},{8,9},{9,8},{10,11... | collective-permute-start | bytes 7077896 | tf_op jit(solution)/shard_map/ppermute | solution.py:623
  73.7 28.4 %collective-permute-start.10 = (bf16[4,48,3072]{2,1,0:T(8,128)(2,1)S(1)}, bf16[4,48,3072]{2,1,0:T(8,128)(2,1)S(1)}, u32[]{:S(2)}, u32[]{:S(2)}) collective-permute-start(bf16[4,48,3072]{2,1,0:T(8,128)(2,1)S(1)} %get-tuple-element.209), channel_id=1, source_target_pairs={{0,2},{1,3},{2,0},{3,1},{4,6},{5,7},{6,4},{7,5},{8,10},{9,11},{10,... | collective-permute-start | bytes 3538952 | tf_op jit(solution)/shard_map/ppermute | solution.py:623
  83.7 3.8 %collective-permute-start.8 = (bf16[8,48,2304]{2,1,0:T(8,128)(2,1)S(1)}, bf16[8,48,2304]{2,1,0:T(8,128)(2,1)S(1)}, u32[]{:S(2)}, u32[]{:S(2)}) collective-permute-start(bf16[8,48,2304]{2,1,0:T(8,128)(2,1)S(1)} %get-tuple-element.189), channel_id=1, source_target_pairs={{0,1},{1,0},{2,3},{3,2},{4,5},{5,4},{6,7},{7,6},{8,9},{9,8},{10,11... | collective-permute-start | bytes 5308424 | tf_op jit(solution)/shard_map/ppermute | solution.py:623
  90.3 4.8 %copy-start.7 = (bf16[1,768,2304]{2,1,0:T(8,128)(2,1)S(1)}, bf16[1,768,2304]{2,1,0:T(8,128)(2,1)}, u32[]{:S(2)}) copy-start(bf16[1,768,2304]{2,1,0:T(8,128)(2,1)} %param.21) | copy-start | bytes 10616836
  90.6 28.4 %collective-permute-start.12 = (bf16[2,192,768]{2,1,0:T(8,128)(2,1)S(1)}, bf16[2,192,768]{2,1,0:T(8,128)(2,1)S(1)}, u32[]{:S(2)}, u32[]{:S(2)}) collective-permute-start(bf16[2,192,768]{2,1,0:T(8,128)(2,1)S(1)} %get-tuple-element.212), channel_id=1, source_target_pairs={{0,8},{1,9},{2,10},{3,11},{4,12},{5,13},{6,14},{7,15},{8,0},{9,1},... | collective-permute-start | bytes 1769480 | tf_op jit(solution)/shard_map/ppermute | solution.py:623
  95.0 3.0 %collective-permute-start.9 = (bf16[8,48,896]{2,1,0:T(8,128)(2,1)S(1)}, bf16[8,48,896]{2,1,0:T(8,128)(2,1)S(1)}, u32[]{:S(2)}, u32[]{:S(2)}) collective-permute-start(bf16[8,48,896]{2,1,0:T(8,128)(2,1)S(1)} %get-tuple-element.204), channel_id=1, source_target_pairs={{0,1},{1,0},{2,3},{3,2},{4,5},{5,4},{6,7},{7,6},{8,9},{9,8},{10,11... | collective-permute-start | bytes 2064392 | tf_op jit(solution)/shard_map/ppermute | solution.py:623
  102.1 17.1 %collective-permute-start.11 = (bf16[2,48,2304]{2,1,0:T(8,128)(2,1)S(1)}, bf16[2,48,2304]{2,1,0:T(8,128)(2,1)S(1)}, u32[]{:S(2)}, u32[]{:S(2)}) collective-permute-start(bf16[2,48,2304]{2,1,0:T(8,128)(2,1)S(1)} %get-tuple-element.210), channel_id=1, source_target_pairs={{0,2},{1,3},{2,0},{3,1},{4,6},{5,7},{6,4},{7,5},{8,10},{9,11},{10,... | collective-permute-start | bytes 1327112 | tf_op jit(solution)/shard_map/ppermute | solution.py:623
  103.0 20.3 %collective-permute-start.13 = (bf16[2,48,2304]{2,1,0:T(8,128)(2,1)S(1)}, bf16[2,48,2304]{2,1,0:T(8,128)(2,1)S(1)}, u32[]{:S(2)}, u32[]{:S(2)}) collective-permute-start(bf16[2,48,2304]{2,1,0:T(8,128)(2,1)S(1)} %get-tuple-element.220), channel_id=1, source_target_pairs={{0,2},{1,3},{2,0},{3,1},{4,6},{5,7},{6,4},{7,5},{8,10},{9,11},{10,... | collective-permute-start | bytes 1327112 | tf_op jit(solution)/shard_map/ppermute | solution.py:623
  104.4 22.2 %collective-permute-start.17 = (bf16[1,48,3072]{2,1,0:T(8,128)(2,1)S(1)}, bf16[1,48,3072]{2,1,0:T(8,128)(2,1)S(1)}, u32[]{:S(2)}, u32[]{:S(2)}) collective-permute-start(bf16[1,48,3072]{2,1,0:T(8,128)(2,1)S(1)} %get-tuple-element.232), channel_id=1, source_target_pairs={{0,4},{1,5},{2,6},{3,7},{4,0},{5,1},{6,2},{7,3},{8,12},{9,13},{10,... | collective-permute-start | bytes 884744 | tf_op jit(solution)/shard_map/ppermute | solution.py:623
  105.8 25.8 %collective-permute-start.16 = (bf16[1,48,3072]{2,1,0:T(8,128)(2,1)S(1)}, bf16[1,48,3072]{2,1,0:T(8,128)(2,1)S(1)}, u32[]{:S(2)}, u32[]{:S(2)}) collective-permute-start(bf16[1,48,3072]{2,1,0:T(8,128)(2,1)S(1)} %get-tuple-element.229), channel_id=1, source_target_pairs={{0,4},{1,5},{2,6},{3,7},{4,0},{5,1},{6,2},{7,3},{8,12},{9,13},{10,... | collective-permute-start | bytes 884744 | tf_op jit(solution)/shard_map/ppermute | solution.py:623
  123.3 9.2 %collective-permute-start.15 = (bf16[4,48,896]{2,1,0:T(8,128)(2,1)S(1)}, bf16[4,48,896]{2,1,0:T(8,128)(2,1)S(1)}, u32[]{:S(2)}, u32[]{:S(2)}) collective-permute-start(bf16[4,48,896]{2,1,0:T(8,128)(2,1)S(1)} %get-tuple-element.227), channel_id=1, source_target_pairs={{0,2},{1,3},{2,0},{3,1},{4,6},{5,7},{6,4},{7,5},{8,10},{9,11},{10,... | collective-permute-start | bytes 1032200 | tf_op jit(solution)/shard_map/ppermute | solution.py:623
  124.4 13.4 %collective-permute-start.18 = (bf16[1,48,2304]{2,1,0:T(8,128)(2,1)S(1)}, bf16[1,48,2304]{2,1,0:T(8,128)(2,1)S(1)}, u32[]{:S(2)}, u32[]{:S(2)}) collective-permute-start(bf16[1,48,2304]{2,1,0:T(8,128)(2,1)S(1)} %get-tuple-element.239), channel_id=1, source_target_pairs={{0,4},{1,5},{2,6},{3,7},{4,0},{5,1},{6,2},{7,3},{8,12},{9,13},{10,... | collective-permute-start | bytes 663560 | tf_op jit(solution)/shard_map/ppermute | solution.py:623
  125.9 19.5 %collective-permute-start.14 = (bf16[1,48,2304]{2,1,0:T(8,128)(2,1)S(1)}, bf16[1,48,2304]{2,1,0:T(8,128)(2,1)S(1)}, u32[]{:S(2)}, u32[]{:S(2)}) collective-permute-start(bf16[1,48,2304]{2,1,0:T(8,128)(2,1)S(1)} %get-tuple-element.224), channel_id=1, source_target_pairs={{0,4},{1,5},{2,6},{3,7},{4,0},{5,1},{6,2},{7,3},{8,12},{9,13},{10,... | collective-permute-start | bytes 663560 | tf_op jit(solution)/shard_map/ppermute | solution.py:623
  131.7 16.4 %collective-permute-start.22 = (bf16[1,48,3072]{2,1,0:T(8,128)(2,1)S(1)}, bf16[1,48,3072]{2,1,0:T(8,128)(2,1)S(1)}, u32[]{:S(2)}, u32[]{:S(2)}) collective-permute-start(bf16[1,48,3072]{2,1,0:T(8,128)(2,1)S(1)} %get-tuple-element.250), channel_id=1, source_target_pairs={{0,8},{1,9},{2,10},{3,11},{4,12},{5,13},{6,14},{7,15},{8,0},{9,1},... | collective-permute-start | bytes 884744 | tf_op jit(solution)/shard_map/ppermute | solution.py:623
  132.5 20.5 %collective-permute-start.20 = (bf16[1,192,768]{2,1,0:T(8,128)(2,1)S(1)}, bf16[1,192,768]{2,1,0:T(8,128)(2,1)S(1)}, u32[]{:S(2)}, u32[]{:S(2)}) collective-permute-start(bf16[1,192,768]{2,1,0:T(8,128)(2,1)S(1)} %get-tuple-element.246), channel_id=1, source_target_pairs={{0,2},{1,3},{2,0},{3,1},{4,6},{5,7},{6,4},{7,5},{8,10},{9,11},{10,... | collective-permute-start | bytes 884744 | tf_op jit(solution)/shard_map/ppermute | solution.py:623
  133.5 19.3 %collective-permute-start.21 = (bf16[2,48,896]{2,1,0:T(8,128)(2,1)S(1)}, bf16[2,48,896]{2,1,0:T(8,128)(2,1)S(1)}, u32[]{:S(2)}, u32[]{:S(2)}) collective-permute-start(bf16[2,48,896]{2,1,0:T(8,128)(2,1)S(1)} %get-tuple-element.248), channel_id=1, source_target_pairs={{0,4},{1,5},{2,6},{3,7},{4,0},{5,1},{6,2},{7,3},{8,12},{9,13},{10,... | collective-permute-start | bytes 516104 | tf_op jit(solution)/shard_map/ppermute | solution.py:623
  145.5 13.5 %collective-permute-start.19 = (bf16[1,48,2304]{2,1,0:T(8,128)(2,1)S(1)}, bf16[1,48,2304]{2,1,0:T(8,128)(2,1)S(1)}, u32[]{:S(2)}, u32[]{:S(2)}) collective-permute-start(bf16[1,48,2304]{2,1,0:T(8,128)(2,1)S(1)} %get-tuple-element.243), channel_id=1, source_target_pairs={{0,8},{1,9},{2,10},{3,11},{4,12},{5,13},{6,14},{7,15},{8,0},{9,1},... | collective-permute-start | bytes 663560 | tf_op jit(solution)/shard_map/ppermute | solution.py:623
  152.9 7.8 %collective-permute-start.23 = (bf16[1,48,896]{2,1,0:T(8,128)(2,1)S(1)}, bf16[1,48,896]{2,1,0:T(8,128)(2,1)S(1)}, u32[]{:S(2)}, u32[]{:S(2)}) collective-permute-start(bf16[1,48,896]{2,1,0:T(8,128)(2,1)S(1)} %get-tuple-element.257), channel_id=1, source_target_pairs={{0,8},{1,9},{2,10},{3,11},{4,12},{5,13},{6,14},{7,15},{8,0},{9,1},... | collective-permute-start | bytes 258056 | tf_op jit(solution)/shard_map/ppermute | solution.py:623
where the time goes:
time: 162 us; the launch traced here: 161 us
  Pallas kernels  73.1 us (45%)
  waiting for transfers between devices  51.1 us (32%)
  starting transfers between devices  28.4 us (18%)
  local copies, waits for them, and re-layouts  7.65 us (5%)
    pallas_call x33, Pallas kernels, kernel_call(): pl.pallas_call(body, out_shape=shapes, in_specs=[SM] * smem + [VM] * (len...  73.1 us
    ppermute x24, waiting for transfers between devices, swapped(): return lax.ppermute(value, axis, [(i, i ^ mask) for i in range(count)])  51.1 us
    ppermute x24, starting transfers between devices, swapped(): return lax.ppermute(value, axis, [(i, i ^ mask) for i in range(count)])  28.4 us
    unnamed x48, local copies, waits for them, and re-layouts  7.51 us
  transfers between devices with their start and end apart: 24, of which 14 were waited for; matrix products, arithmetic and copies ran while one was open for 0% of the time, Pallas kernels for 33%

commit v1 on v0

--- a/solution.py
+++ b/solution.py
@@ -17,7 +17,7 @@
 F32 = jnp.float32
 TILE = 32
 
-COSTS = {"first_back": 3 * 10**10, "attention_back_4": 3 * 10**10, "input_back": 3 * 10**10}
+COSTS = {"proj": 3 * 10**9, "cls": 3 * 10**9, "attention": 8 * 10**9, "first": 2 * 10**9, "inner": 6 * 10**9, "second": 4 * 10**9, "first_back": 3 * 10**10, "attention_back_4": 3 * 10**10, "input_back": 3 * 10**10}
 
 VM = pl.BlockSpec(memory_space=pltpu.VMEM)
 SM = pl.BlockSpec(memory_space=pltpu.SMEM)
@@ -119,7 +119,12 @@
     return (place == wanted).astype(F32)
 
 
-def cls_kernel(place, seg, x, proj, w_out, b_out, g1, b1, w_in, b_in, w_back, b_back, g2, b2, cls):
+def cls_kernel(place, seg, x, proj, w_out, w_in, w_back, *refs):
+    vectors, (cls, *held, sems) = refs[:7], refs[7:]
+    copies = [pltpu.make_async_copy(a, b, sems.at[k]) for k, (a, b) in enumerate(zip(vectors, held))]
+    for copy in copies:
+        copy.start()
+    b_out, g1, b1, b_in, b_back, g2, b2 = held
     length, width = x.shape
     count = cls.shape[0]
     heads = width // HEAD_DIM
@@ -143,6 +148,8 @@
     attended = jnp.zeros((count, width), F32)
     for h in range(heads):
         attended = attended + jnp.where(lane_head == h, mixed[h * count : (h + 1) * count], 0.0)
+    for copy in copies:
+        copy.wait()
     first = x_cls + (nn(attended.astype(BF), w_out[...]) + b_out[...])
     normed = normalise(first)[0] * g1[...] + b1[...]
     inner = nn(normed.astype(BF), w_in[...]) + b_in[...]
@@ -373,26 +380,23 @@
         sums[:, cols] = jnp.sum(value.astype(F32), 0, keepdims=True)
         return carry
 
-    lax.fori_loop(0, w_back.shape[0] // block, step, 0, unroll=2)
-
-
-def first_back_kernel(inner, w_in, grad_second, n1, r1, g1, w_out, grad, low, att, sums, work):
+    lax.fori_loop(0, w_back.shape[0] // block, step, 0, unroll=4)
+
+
+def first_back_kernel(inner, w_in, grad_second, n1, r1, g1, w_out, grad, low, att, sums, work_a, work_b):
     length, width = grad_second.shape
-    part = work.shape[0]
-
-    def back_part(k, totals):
-        at = pl.multiple_of(k * part, part)
-        work[...] = nt(inner[pl.ds(at, part), :], w_in[...])
+    part = length // 2
+    works = (work_a, work_b)
+    for k in range(2):
+        works[k][...] = nt(inner[k * part : (k + 1) * part, :], w_in[...])
+    totals = None
+    for k in range(2):
         for r in range(0, part, TILE):
-            rows = pl.ds(pl.multiple_of(at + r, TILE), TILE)
-            value = grad_second[rows, :] + work[r : r + TILE, :]
+            rows = slice(k * part + r, k * part + r + TILE)
+            value = grad_second[rows, :] + works[k][r : r + TILE, :]
             totals = norm_back_rows(rows, value, n1, r1, g1, grad, low, totals)
-        rows = pl.ds(at, part)
+        rows = slice(k * part, (k + 1) * part)
         att[rows, :] = nt(low[rows, :], w_out[...]).astype(BF)
-        return totals
-
-    zero = jnp.zeros((8, width), F32)
-    totals = lax.fori_loop(0, length // part, back_part, (zero, zero, zero))
     for k, total in enumerate(totals):
         sums[k : k + 1, :] = jnp.sum(total, 0, keepdims=True)
 
@@ -713,8 +717,13 @@
     )
     cls = kernel_call(
         cls_kernel, sds((count, width), BF),
-        [place, seg_ids, x, proj, w_out, b_out, ln1_gain, ln1_bias, w_in, b_in, w_back, b_back,
-         ln2_gain, ln2_bias],
+        [place, seg_ids, x, proj, w_out, w_in, w_back] + [
+            pltpu.with_memory_space_constraint(member, pltpu.HBM)
+            for member in (b_out, ln1_gain, ln1_bias, b_in, b_back, ln2_gain, ln2_bias)
+        ],
+        hbm=7,
+        scratch=[pltpu.VMEM((1, width), F32)] * 3 + [pltpu.VMEM((1, hidden), F32)]
+        + [pltpu.VMEM((1, width), F32)] * 3 + [pltpu.SemaphoreType.DMA((7,))],
         smem=1, mib=3, flops=2 * 256 * width * hidden * 2, name="cls",
     )
     other = swapped(cls, "tower", 1)
@@ -785,7 +794,7 @@
     inner_call = dict(mib=3, flops=2 * length * width * hidden, name="inner_back")
     inner_shape = [sds((length, hidden), BF), sds((1, hidden), F32)]
     first_call = dict(
-        scratch=[half_work], mib=5, flops=2 * length * width * (hidden + width), name="first_back"
+        scratch=[half_work] * 2, mib=5, flops=2 * length * width * (hidden + width), name="first_back"
     )
     first_shape = [
         sds((length, width), F32), sds((length, width), BF), sds((length, width), BF), sds((8, width), F32)

time: 162 us -> 158 us (0.975)
  waiting for transfers between devices: 51.1 us -> 56.5 us
  starting transfers between devices: 28.4 us -> 24 us
  local copies, waits for them, and re-layouts: 7.65 us -> 4.44 us
    ppermute x24, waiting for transfers between devices: 51.1 us -> 56.5 us  [swapped(): return lax.ppermute(value, axis, [(i, i ^ mask) for i in range(count)])]
    ppermute x24, starting transfers between devices: 28.4 us -> 24 us  [swapped(): return lax.ppermute(value, axis, [(i, i ^ mask) for i in range(count)])]
    unnamed x48 -> x44, local copies, waits for them, and re-layouts: 7.51 us -> 4.29 us
  transfers between devices with their start and end apart: 24 -> 24, of which waited for: 14 -> 16; matrix products, arithmetic and copies ran while one was open for 0% -> 0% of each run, Pallas kernels for 33% -> 32%
where the time goes in v1:
time: 158 us
  Pallas kernels  71.8 us (45%)
  waiting for transfers between devices  56.5 us (36%)
  starting transfers between devices  24 us (15%)
  local copies, waits for them, and re-layouts  4.44 us (3%)
    pallas_call x33, Pallas kernels, kernel_call(): pl.pallas_call(body, out_shape=shapes, in_specs=[SM] * smem + [VM] * (len...  71.8 us
    ppermute x24, waiting for transfers between devices, swapped(): return lax.ppermute(value, axis, [(i, i ^ mask) for i in range(count)])  56.5 us
    ppermute x24, starting transfers between devices, swapped(): return lax.ppermute(value, axis, [(i, i ^ mask) for i in range(count)])  24 us
    unnamed x44, local copies, waits for them, and re-layouts  4.29 us
  transfers between devices with their start and end apart: 24, of which 16 were waited for; matrix products, arithmetic and copies ran while one was open for 0% of the time, Pallas kernels for 32%

profile of v1, /device:TPU:0, one launch (start us, length us, event | category | flops | bytes accessed | tf_op | source)
XLA Modules:
  0.0 157.9 jit_solution(2614866106240459446)
XLA Ops:
  0.7 4.7 %proj.1 = bf16[512,2304]{1,0:T(8,128)(2,1)S(1)} custom-call(bf16[512,768]{1,0:T(8,128)(2,1)} %bitcast.23, bf16[768,2304]{1,0:T(8,128)(2,1)} %bitcast.39, f32[1,768]{1,0:T(1,128)} %bq_hbm.1, f32[1,768]{1,0:T(1,128)} %bv_hbm.1), custom_call_target="tpu_custom_call" | custom-call | flops 3000000000 | tf_op jit(solution)/shard_map/proj/pallas_call | solution.py:42
  6.1 1.3 copy-done.3
  7.3 4.6 %cls.1 = bf16[16,768]{1,0:T(8,128)(2,1)S(1)} custom-call(s32[2]{0:T(128)S(1)} %pad_add_fusion.place, s32[1,512]{1,0:T(1,128)S(1)} %copy-done.6, bf16[512,768]{1,0:T(8,128)(2,1)S(1)} %bitcast.24, bf16[512,2304]{1,0:T(8,128)(2,1)S(1)} %proj.1, bf16[768,768]{1,0:T(8,128)(2,1)S(1)} %bitcast.33, bf16[768,3072]{1,0:T(8,128)(2,1)S(1)} %bitcast.28, ...), custom_call_target="tpu_custom_call" | custom-call | flops 3000000000 | tf_op jit(solution)/shard_map/cls/pallas_call | solution.py:42
  11.9 3.0 %collective-permute-start = (bf16[16,768]{1,0:T(8,128)(2,1)S(1)}, bf16[16,768]{1,0:T(8,128)(2,1)S(1)}, u32[]{:S(2)}, u32[]{:S(2)}) collective-permute-start(bf16[16,768]{1,0:T(8,128)(2,1)S(1)} %cls.1), channel_id=1, source_target_pairs={{0,16},{16,0},{1,17},{17,1},{2,18},{18,2},{3,19},{19,3},{4,20},{20... | collective-permute-start | bytes 73736 | tf_op jit(solution)/shard_map/ppermute | solution.py:627
  15.2 7.0 %attention.1 = (bf16[512,768]{1,0:T(8,128)(2,1)S(1)}, bf16[12,512,512]{2,1,0:T(8,128)(2,1)S(1)}) custom-call(s32[2]{0:T(128)S(1)} %pad_add_fusion.place, s32[1,512]{1,0:T(1,128)S(1)} %copy-done.6, s32[512,1]{1,0:T(8,128)S(1)} %copy.32.seg_col, bf16[512,2304]{1,0:T(8,128)(2,1)S(1)} %proj.1), custom_call_target="tpu_custom_call" | custom-call | flops 8000000000 | tf_op jit(solution)/shard_map/attention/pallas_call | solution.py:42
  22.8 2.7 %collective-permute-start.1 = (bf16[24,768]{1,0:T(8,128)(2,1)S(1)}, bf16[24,768]{1,0:T(8,128)(2,1)S(1)}, u32[]{:S(2)}, u32[]{:S(2)}) collective-permute-start(bf16[24,768]{1,0:T(8,128)(2,1)S(1)} %packet.1), channel_id=1, source_target_pairs={{0,8},{1,9},{2,10},{3,11},{4,12},{5,13},{6,14},{7,15},{8,0},{9,1},... | collective-permute-start | bytes 110600 | tf_op jit(solution)/shard_map/ppermute | solution.py:627
  25.4 1.7 %first.1 = (f32[512,768]{1,0:T(8,128)S(1)}, f32[512,1]{1,0:T(8,128)S(1)}, bf16[512,768]{1,0:T(8,128)(2,1)S(1)}) custom-call(bf16[512,768]{1,0:T(8,128)(2,1)S(1)} %bitcast.25, bf16[512,768]{1,0:T(8,128)(2,1)S(1)} %get-tuple-element.145.attended.refs_2_, bf16[768,768]{1,0:T(8,128)(2,1)S(1)} %bitcast.34, f32[1,768]{1,0:T(1,128)S(1)} %copy-done.9, ...), custom_call_target="tpu_custom_call" | custom-call | flops 2000000000 | tf_op jit(solution)/shard_map/first/pallas_call | solution.py:42
  27.7 1.6 %collective-permute-start.2 = (bf16[48,768]{1,0:T(8,128)(2,1)S(1)}, bf16[48,768]{1,0:T(8,128)(2,1)S(1)}, u32[]{:S(2)}, u32[]{:S(2)}) collective-permute-start(bf16[48,768]{1,0:T(8,128)(2,1)S(1)} %pad_maximum_fusion.2), channel_id=1, source_target_pairs={{0,4},{1,5},{2,6},{3,7},{4,0},{5,1},{6,2},{7,3},{8,12},{9,13},{10,... | collective-permute-start | bytes 221192 | tf_op jit(solution)/shard_map/ppermute | solution.py:627
  29.4 2.3 %copy-done.2 = bf16[1,768,3072]{2,1,0:T(8,128)(2,1)S(1)} copy-done((bf16[1,768,3072]{2,1,0:T(8,128)(2,1)S(1)}, bf16[1,768,3072]{2,1,0:T(8,128)(2,1)}, u32[]{:S(2)}) %copy-start.2) | copy-done | bytes 4718616
  31.7 6.0 %inner.1 = (bf16[512,3072]{1,0:T(8,128)(2,1)S(1)}, bf16[512,3072]{1,0:T(8,128)(2,1)S(1)}) custom-call(bf16[512,768]{1,0:T(8,128)(2,1)S(1)} %get-tuple-element.148.low.refs_0_, bf16[768,3072]{1,0:T(8,128)(2,1)S(1)} %bitcast.29, f32[1,3072]{1,0:T(1,128)S(1)} %copy-done.8), custom_call_target="tpu_custom_call" | custom-call | flops 6000000000 | tf_op jit(solution)/shard_map/inner/pallas_call | solution.py:42
  37.7 1.6 collective-permute-start.3
  39.3 4.2 %second.1 = (f32[512,768]{1,0:T(8,128)S(1)}, f32[512,1]{1,0:T(8,128)S(1)}, bf16[512,768]{1,0:T(8,128)(2,1)}) custom-call(bf16[512,3072]{1,0:T(8,128)(2,1)S(1)} %get-tuple-element.151.act.refs_0_, bf16[3072,768]{1,0:T(8,128)(2,1)S(1)} %bitcast.21, f32[1,768]{1,0:T(1,128)S(1)} %copy-done.11, f32[512,768]{1,0:T(8,128)S(1)} %get-tuple-element.152.n1, ...), custom_call_target="tpu_custom_call" | custom-call | flops 4000000000 | tf_op jit(solution)/shard_map/second/pallas_call | solution.py:42
  43.6 1.6 collective-permute-done.4.far
  45.2 3.3 %loss.1.cls_grad = f32[16,768]{1,0:T(8,128)S(1)} custom-call(s32[2]{0:T(128)S(1)} %pad_add_fusion.place, bf16[192,768]{1,0:T(8,128)(2,1)S(1)} %pad_maximum_fusion.near, bf16[192,768]{1,0:T(8,128)(2,1)S(1)} %collective-permute-done.4.far), custom_call_target="tpu_custom_call" | custom-call | tf_op jit(solution)/shard_map/loss/pallas_call | solution.py:42
  48.4 1.9 %second_back.1 = (f32[512,768]{1,0:T(8,128)S(1)}, bf16[512,768]{1,0:T(8,128)(2,1)S(1)}, f32[8,768]{1,0:T(8,128)S(1)}) custom-call(s32[2]{0:T(128)S(1)} %pad_add_fusion.place, s32[1,512]{1,0:T(1,128)S(1)} %copy-done.6, bf16[512,768]{1,0:T(8,128)(2,1)S(1)} %bitcast.36, f32[16,768]{1,0:T(8,128)S(1)} %loss.1.cls_grad, f32[512,768]{1,0:T(8,128)S(1)} %get-tuple-element.156.n2, ...), custom_call_target="tpu_custom_call" | custom-call | tf_op jit(solution)/shard_map/second_back/pallas_call | solution.py:42
  50.4 4.3 %grad_w_back.1 = (bf16[8,192,768]{2,1,0:T(8,128)(2,1)S(1)}, bf16[8,192,768]{2,1,0:T(8,128)(2,1)S(1)}) custom-call(s32[2]{0:T(128)S(1)} %pad_add_fusion.place, bf16[512,3072]{1,0:T(8,128)(2,1)S(1)} %get-tuple-element.151.act.refs_0_, bf16[512,768]{1,0:T(8,128)(2,1)S(1)} %get-tuple-element.160.refs_1_.low), custom_call_target="tpu_custom_call" | custom-call | tf_op jit(solution)/shard_map/grad_w_back/pallas_call | solution.py:42
  54.9 3.5 %inner_back.1 = (bf16[512,3072]{1,0:T(8,128)(2,1)S(1)}, f32[1,3072]{1,0:T(1,128)S(1)}) custom-call(bf16[512,768]{1,0:T(8,128)(2,1)S(1)} %get-tuple-element.160.refs_1_.low, bf16[3072,768]{1,0:T(8,128)(2,1)S(1)} %bitcast.22, bf16[512,3072]{1,0:T(8,128)(2,1)S(1)} %get-tuple-element.161.slope), custom_call_target="tpu_custom_call" | custom-call | tf_op jit(solution)/shard_map/inner_back/pallas_call | solution.py:42
  58.4 0.9 collective-permute-done.5.refs_1_
  60.6 4.4 %grad_w_in.1 = (bf16[8,48,3072]{2,1,0:T(8,128)(2,1)S(1)}, bf16[8,48,3072]{2,1,0:T(8,128)(2,1)S(1)}) custom-call(s32[2]{0:T(128)S(1)} %pad_add_fusion.place, bf16[512,768]{1,0:T(8,128)(2,1)S(1)} %get-tuple-element.148.low.refs_0_, bf16[512,3072]{1,0:T(8,128)(2,1)S(1)} %get-tuple-element.169.refs_1_.inner), custom_call_target="tpu_custom_call" | custom-call | tf_op jit(solution)/shard_map/grad_w_in/pallas_call | solution.py:42
  65.1 4.0 %first_back.1 = (f32[512,768]{1,0:T(8,128)S(1)}, bf16[512,768]{1,0:T(8,128)(2,1)S(1)}, bf16[512,768]{1,0:T(8,128)(2,1)S(1)}, f32[8,768]{1,0:T(8,128)S(1)}) custom-call(bf16[512,3072]{1,0:T(8,128)(2,1)S(1)} %get-tuple-element.169.refs_1_.inner, bf16[768,3072]{1,0:T(8,128)(2,1)S(1)} %bitcast.32, f32[512,768]{1,0:T(8,128)S(1)} %get-tuple-element.170.grad_second, ...), custom_call_target="tpu_custom_call" | custom-call | flops 30000001024 | tf_op jit(solution)/shard_map/first_back/pallas_call | solution.py:42
  70.2 1.0 collective-permute-start.10
  71.1 5.6 %attention_back_0.1 = (bf16[512,1536]{1,0:T(8,128)(2,1)S(1)}, f32[1,1536]{1,0:T(1,128)S(1)}) custom-call(bf16[512,2304]{1,0:T(8,128)(2,1)S(1)} %proj.1, bf16[12,512,512]{2,1,0:T(8,128)(2,1)S(1)} %get-tuple-element.154.probs, bf16[512,768]{1,0:T(8,128)(2,1)S(1)} %get-tuple-element.184.att_grad), custom_call_target="tpu_custom_call" | custom-call | tf_op jit(solution)/shard_map/attention_back_0/pallas_call | solution.py:42
  76.7 3.5 %grad_w_qkv_1.1 = (bf16[8,48,2304]{2,1,0:T(8,128)(2,1)S(1)}, bf16[8,48,2304]{2,1,0:T(8,128)(2,1)S(1)}) custom-call(s32[2]{0:T(128)S(1)} %pad_add_fusion.place, bf16[512,768]{1,0:T(8,128)(2,1)S(1)} %bitcast.26, bf16[512,1536]{1,0:T(8,128)(2,1)S(1)} %get-tuple-element.180.refs_1_.left, bf16[512,768]{1,0:T(8,128)(2,1)S(1)} %get-tuple-element.145.attended.refs_2_, ...), custom_call_target="tpu_custom_call" | custom-call | tf_op jit(solution)/shard_map/grad_w_qkv_1/pallas_call | solution.py:42
  80.3 2.7 %attention_back_4.1 = (bf16[512,768]{1,0:T(8,128)(2,1)S(1)}, f32[1,768]{1,0:T(1,128)S(1)}) custom-call(bf16[512,2304]{1,0:T(8,128)(2,1)S(1)} %proj.1, bf16[12,512,512]{2,1,0:T(8,128)(2,1)S(1)} %get-tuple-element.154.probs, bf16[512,768]{1,0:T(8,128)(2,1)S(1)} %get-tuple-element.184.att_grad), custom_call_target="tpu_custom_call" | custom-call | flops 30000001024 | tf_op jit(solution)/shard_map/attention_back_4/pallas_call | solution.py:42
  83.0 1.0 collective-permute-done.8.refs_1_
  84.4 3.5 %collective-permute-done.7.refs_1_ = bf16[4,192,768]{2,1,0:T(8,128)(2,1)S(1)} collective-permute-done((bf16[4,192,768]{2,1,0:T(8,128)(2,1)S(1)}, bf16[4,192,768]{2,1,0:T(8,128)(2,1)S(1)}, u32[]{:S(2)}, u32[]{:S(2)}) %collective-permute-start.7) | collective-permute-done | bytes 1179680 | tf_op jit(solution)/shard_map/ppermute | solution.py:627
  88.2 2.9 %collective-permute-start.12 = (bf16[2,192,768]{2,1,0:T(8,128)(2,1)S(1)}, bf16[2,192,768]{2,1,0:T(8,128)(2,1)S(1)}, u32[]{:S(2)}, u32[]{:S(2)}) collective-permute-start(bf16[2,192,768]{2,1,0:T(8,128)(2,1)S(1)} %get-tuple-element.212), channel_id=1, source_target_pairs={{0,8},{1,9},{2,10},{3,11},{4,12},{5,13},{6,14},{7,15},{8,0},{9,1},... | collective-permute-start | bytes 1769480 | tf_op jit(solution)/shard_map/ppermute | solution.py:627
  91.1 1.5 grad_w_qkv_2.1
  92.7 2.9 %input_back.1 = bf16[512,768]{1,0:T(8,128)(2,1)} custom-call(bf16[512,1536]{1,0:T(8,128)(2,1)S(1)} %get-tuple-element.180.refs_1_.left, bf16[512,768]{1,0:T(8,128)(2,1)S(1)} %get-tuple-element.201.grad_proj.right, bf16[768,2304]{1,0:T(8,128)(2,1)S(1)} %bitcast.40, f32[512,768]{1,0:T(8,128)S(1)} %get-tuple-element.175.grad_first), custom_call_target="tpu_custom_call" | custom-call | flops 30000001024 | tf_op jit(solution)/shard_map/input_back/pallas_call | solution.py:42
  95.8 2.5 %collective-permute-done.10.refs_1_ = bf16[4,48,3072]{2,1,0:T(8,128)(2,1)S(1)} collective-permute-done((bf16[4,48,3072]{2,1,0:T(8,128)(2,1)S(1)}, bf16[4,48,3072]{2,1,0:T(8,128)(2,1)S(1)}, u32[]{:S(2)}, u32[]{:S(2)}) %collective-permute-start.10) | collective-permute-done | bytes 1179680 | tf_op jit(solution)/shard_map/ppermute | solution.py:627
  98.2 0.9 collective-permute-start.11
  99.2 1.1 collective-permute-start.13
  100.5 1.4 collective-permute-start.17
  102.6 14.0 %collective-permute-done.12.refs_1_ = bf16[2,192,768]{2,1,0:T(8,128)(2,1)S(1)} collective-permute-done((bf16[2,192,768]{2,1,0:T(8,128)(2,1)S(1)}, bf16[2,192,768]{2,1,0:T(8,128)(2,1)S(1)}, u32[]{:S(2)}, u32[]{:S(2)}) %collective-permute-start.12) | collective-permute-done | bytes 589856 | tf_op jit(solution)/shard_map/ppermute | solution.py:627
  116.7 2.4 %collective-permute-done.13.refs_2_ = bf16[2,48,2304]{2,1,0:T(8,128)(2,1)S(1)} collective-permute-done((bf16[2,48,2304]{2,1,0:T(8,128)(2,1)S(1)}, bf16[2,48,2304]{2,1,0:T(8,128)(2,1)S(1)}, u32[]{:S(2)}, u32[]{:S(2)}) %collective-permute-start.13) | collective-permute-done | bytes 442400 | tf_op jit(solution)/shard_map/ppermute | solution.py:627
  119.1 0.9 collective-permute-start.15
  120.2 1.4 collective-permute-start.18
  123.0 7.5 %collective-permute-done.16.refs_1_ = bf16[1,48,3072]{2,1,0:T(8,128)(2,1)S(1)} collective-permute-done((bf16[1,48,3072]{2,1,0:T(8,128)(2,1)S(1)}, bf16[1,48,3072]{2,1,0:T(8,128)(2,1)S(1)}, u32[]{:S(2)}, u32[]{:S(2)}) %collective-permute-start.16) | collective-permute-done | bytes 294944 | tf_op jit(solution)/shard_map/ppermute | solution.py:627
  130.7 1.2 collective-permute-start.20
  132.0 0.8 collective-permute-start.21
  132.8 5.9 %collective-permute-done.18.refs_2_ = bf16[1,48,2304]{2,1,0:T(8,128)(2,1)S(1)} collective-permute-done((bf16[1,48,2304]{2,1,0:T(8,128)(2,1)S(1)}, bf16[1,48,2304]{2,1,0:T(8,128)(2,1)S(1)}, u32[]{:S(2)}, u32[]{:S(2)}) %collective-permute-start.18) | collective-permute-done | bytes 221216 | tf_op jit(solution)/shard_map/ppermute | solution.py:627
  138.7 6.1 %collective-permute-done.14.refs_1_ = bf16[1,48,2304]{2,1,0:T(8,128)(2,1)S(1)} collective-permute-done((bf16[1,48,2304]{2,1,0:T(8,128)(2,1)S(1)}, bf16[1,48,2304]{2,1,0:T(8,128)(2,1)S(1)}, u32[]{:S(2)}, u32[]{:S(2)}) %collective-permute-start.14) | collective-permute-done | bytes 221216 | tf_op jit(solution)/shard_map/ppermute | solution.py:627
  145.1 0.9 finish.2
  145.9 3.0 %collective-permute-done.21.refs_1_ = bf16[2,48,896]{2,1,0:T(8,128)(2,1)S(1)} collective-permute-done((bf16[2,48,896]{2,1,0:T(8,128)(2,1)S(1)}, bf16[2,48,896]{2,1,0:T(8,128)(2,1)S(1)}, u32[]{:S(2)}, u32[]{:S(2)}) %collective-permute-start.21) | collective-permute-done | bytes 172064 | tf_op jit(solution)/shard_map/ppermute | solution.py:627
  149.6 0.9 finish.3
  150.5 5.5 %collective-permute-done.19.came = bf16[1,48,2304]{2,1,0:T(8,128)(2,1)S(1)} collective-permute-done((bf16[1,48,2304]{2,1,0:T(8,128)(2,1)S(1)}, bf16[1,48,2304]{2,1,0:T(8,128)(2,1)S(1)}, u32[]{:S(2)}, u32[]{:S(2)}) %collective-permute-start.19) | collective-permute-done | bytes 221216 | tf_op jit(solution)/shard_map/ppermute | solution.py:627
  156.1 0.9 collective-permute-done.23.came_last
  157.0 0.9 finish_last.1
  (85 shorter events, 9.5 us)
Async XLA Ops:
  0.7 4.7 %slice-start = ((s8[4718592]{0:T(1024)(128)(4,1)}), s8[4194304]{0:T(1024)(128)(4,1)S(1)}, s32[]{:S(2)}) async-start(s8[4718592]{0:T(1024)(128)(4,1)} %bitcast.16), calls=%async_computation | async-start | bytes 8388608
  0.7 4.7 %slice-start.1 = ((s8[4718592]{0:T(1024)(128)(4,1)}), s8[524288]{0:T(1024)(128)(4,1)S(1)}, s32[]{:S(2)}) async-start(s8[4718592]{0:T(1024)(128)(4,1)} %bitcast.16), calls=%async_computation.1 | async-start | bytes 1048576
  0.7 4.7 %copy-start = (bf16[1,512,768]{2,1,0:T(8,128)(2,1)S(1)}, bf16[1,512,768]{2,1,0:T(8,128)(2,1)}, u32[]{:S(2)}) copy-start(bf16[1,512,768]{2,1,0:T(8,128)(2,1)} %param.17) | copy-start | bytes 2359300
  0.7 5.3 %copy-start.1 = (bf16[1,768,3072]{2,1,0:T(8,128)(2,1)S(1)}, bf16[1,768,3072]{2,1,0:T(8,128)(2,1)}, u32[]{:S(2)}) copy-start(bf16[1,768,3072]{2,1,0:T(8,128)(2,1)} %param.28) | copy-start | bytes 14155780
  0.7 5.3 %copy-start.6 = (s32[1,512]{1,0:T(1,128)S(1)}, s32[1,512]{1,0:T(1,128)}, u32[]{:S(2)}) copy-start(s32[1,512]{1,0:T(1,128)} %seg.3) | copy-start | bytes 6148
  6.1 1.3 copy-start.3
  11.9 10.3 %collective-permute-start = (bf16[16,768]{1,0:T(8,128)(2,1)S(1)}, bf16[16,768]{1,0:T(8,128)(2,1)S(1)}, u32[]{:S(2)}, u32[]{:S(2)}) collective-permute-start(bf16[16,768]{1,0:T(8,128)(2,1)S(1)} %cls.1), channel_id=1, source_target_pairs={{0,16},{16,0},{1,17},{17,1},{2,18},{18,2},{3,19},{19,3},{4,20},{20... | collective-permute-start | bytes 73736 | tf_op jit(solution)/shard_map/ppermute | solution.py:627
  15.1 7.1 %copy-start.14 = (s32[16]{0:T(128)S(1)}, s32[16]{0:T(128)}, u32[]{:S(2)}) copy-start(s32[16]{0:T(128)} %param.19) | copy-start | bytes 196
  15.1 10.3 %copy-start.4 = (bf16[1,768,768]{2,1,0:T(8,128)(2,1)S(1)}, bf16[1,768,768]{2,1,0:T(8,128)(2,1)}, u32[]{:S(2)}) copy-start(bf16[1,768,768]{2,1,0:T(8,128)(2,1)} %param.24) | copy-start | bytes 3538948
  15.1 10.3 %copy-start.9 = (f32[1,768]{1,0:T(1,128)S(1)}, f32[1,768]{1,0:T(1,128)}, u32[]{:S(2)}) copy-start(f32[1,768]{1,0:T(1,128)} %b_out.1) | copy-start | bytes 9220
  15.1 10.3 %copy-start.10 = (f32[1,768]{1,0:T(1,128)S(1)}, f32[1,768]{1,0:T(1,128)}, u32[]{:S(2)}) copy-start(f32[1,768]{1,0:T(1,128)} %b1.3) | copy-start | bytes 9220
  15.1 10.3 %copy-start.13 = (f32[1,768]{1,0:T(1,128)S(1)}, f32[1,768]{1,0:T(1,128)}, u32[]{:S(2)}) copy-start(f32[1,768]{1,0:T(1,128)} %g1.5) | copy-start | bytes 9220
  22.7 6.6 %copy-start.8 = (f32[1,3072]{1,0:T(1,128)S(1)}, f32[1,3072]{1,0:T(1,128)}, u32[]{:S(2)}) copy-start(f32[1,3072]{1,0:T(1,128)} %b_in.1) | copy-start | bytes 36868
  22.8 4.9 %collective-permute-start.1 = (bf16[24,768]{1,0:T(8,128)(2,1)S(1)}, bf16[24,768]{1,0:T(8,128)(2,1)S(1)}, u32[]{:S(2)}, u32[]{:S(2)}) collective-permute-start(bf16[24,768]{1,0:T(8,128)(2,1)S(1)} %packet.1), channel_id=1, source_target_pairs={{0,8},{1,9},{2,10},{3,11},{4,12},{5,13},{6,14},{7,15},{8,0},{9,1},... | collective-permute-start | bytes 110600 | tf_op jit(solution)/shard_map/ppermute | solution.py:627
  27.7 11.6 %slice-start.2 = ((s8[4718592]{0:T(1024)(128)(4,1)}), s8[4194304]{0:T(1024)(128)(4,1)S(1)}, s32[]{:S(2)}) async-start(s8[4718592]{0:T(1024)(128)(4,1)} %bitcast.19), calls=%async_computation.2 | async-start | bytes 8388608
  27.7 11.6 %slice-start.3 = ((s8[4718592]{0:T(1024)(128)(4,1)}), s8[524288]{0:T(1024)(128)(4,1)S(1)}, s32[]{:S(2)}) async-start(s8[4718592]{0:T(1024)(128)(4,1)} %bitcast.19), calls=%async_computation.3 | async-start | bytes 1048576
  27.7 10.0 %collective-permute-start.2 = (bf16[48,768]{1,0:T(8,128)(2,1)S(1)}, bf16[48,768]{1,0:T(8,128)(2,1)S(1)}, u32[]{:S(2)}, u32[]{:S(2)}) collective-permute-start(bf16[48,768]{1,0:T(8,128)(2,1)S(1)} %pad_maximum_fusion.2), channel_id=1, source_target_pairs={{0,4},{1,5},{2,6},{3,7},{4,0},{5,1},{6,2},{7,3},{8,12},{9,13},{10,... | collective-permute-start | bytes 221192 | tf_op jit(solution)/shard_map/ppermute | solution.py:627
  29.4 2.3 %copy-start.2 = (bf16[1,768,3072]{2,1,0:T(8,128)(2,1)S(1)}, bf16[1,768,3072]{2,1,0:T(8,128)(2,1)}, u32[]{:S(2)}) copy-start(bf16[1,768,3072]{2,1,0:T(8,128)(2,1)} %param.28) | copy-start | bytes 14155780
  31.7 7.6 %copy-start.7 = (f32[1,768]{1,0:T(1,128)S(1)}, f32[1,768]{1,0:T(1,128)}, u32[]{:S(2)}) copy-start(f32[1,768]{1,0:T(1,128)} %g2.3) | copy-start | bytes 9220
  31.7 7.6 %copy-start.11 = (f32[1,768]{1,0:T(1,128)S(1)}, f32[1,768]{1,0:T(1,128)}, u32[]{:S(2)}) copy-start(f32[1,768]{1,0:T(1,128)} %b_back.1) | copy-start | bytes 9220
  31.7 7.6 %copy-start.12 = (f32[1,768]{1,0:T(1,128)S(1)}, f32[1,768]{1,0:T(1,128)}, u32[]{:S(2)}) copy-start(f32[1,768]{1,0:T(1,128)} %b2.1) | copy-start | bytes 9220
  37.7 5.8 %collective-permute-start.3 = (bf16[96,768]{1,0:T(8,128)(2,1)S(1)}, bf16[96,768]{1,0:T(8,128)(2,1)S(1)}, u32[]{:S(2)}, u32[]{:S(2)}) collective-permute-start(bf16[96,768]{1,0:T(8,128)(2,1)S(1)} %pad_maximum_fusion.1), channel_id=1, source_target_pairs={{0,2},{1,3},{2,0},{3,1},{4,6},{5,7},{6,4},{7,5},{8,10},{9,11},{10,... | collective-permute-start | bytes 442376 | tf_op jit(solution)/shard_map/ppermute | solution.py:627
  43.5 4.9 %copy-start.5 = (bf16[1,512,768]{2,1,0:T(8,128)(2,1)S(1)}, bf16[1,512,768]{2,1,0:T(8,128)(2,1)}, u32[]{:S(2)}) copy-start(bf16[1,512,768]{2,1,0:T(8,128)(2,1)} %param.20) | copy-start | bytes 2359300
  43.5 1.6 %collective-permute-start.4 = (bf16[192,768]{1,0:T(8,128)(2,1)S(1)}, bf16[192,768]{1,0:T(8,128)(2,1)S(1)}, u32[]{:S(2)}, u32[]{:S(2)}) collective-permute-start(bf16[192,768]{1,0:T(8,128)(2,1)S(1)} %pad_maximum_fusion.near), channel_id=1, source_target_pairs={{0,1},{1,0},{2,3},{3,2},{4,5},{5,4},{6,7},{7,6},{8,9},{9,8},{10,11... | collective-permute-start | bytes 884744 | tf_op jit(solution)/shard_map/ppermute | solution.py:627
  54.7 4.6 %collective-permute-start.5 = (bf16[8,192,768]{2,1,0:T(8,128)(2,1)S(1)}, bf16[8,192,768]{2,1,0:T(8,128)(2,1)S(1)}, u32[]{:S(2)}, u32[]{:S(2)}) collective-permute-start(bf16[8,192,768]{2,1,0:T(8,128)(2,1)S(1)} %get-tuple-element.164), channel_id=1, source_target_pairs={{0,1},{1,0},{2,3},{3,2},{4,5},{5,4},{6,7},{7,6},{8,9},{9,8},{10,11... | collective-permute-start | bytes 7077896 | tf_op jit(solution)/shard_map/ppermute | solution.py:627
  54.9 10.2 %slice-start.4 = ((s8[4718592]{0:T(1024)(128)(4,1)}), s8[4194304]{0:T(1024)(128)(4,1)S(1)}, s32[]{:S(2)}) async-start(s8[4718592]{0:T(1024)(128)(4,1)} %bitcast.30), calls=%async_computation.4 | async-start | bytes 8388608
  59.3 5.8 %slice-start.5 = ((s8[4718592]{0:T(1024)(128)(4,1)}), s8[524288]{0:T(1024)(128)(4,1)S(1)}, s32[]{:S(2)}) async-start(s8[4718592]{0:T(1024)(128)(4,1)} %bitcast.30), calls=%async_computation.5 | async-start | bytes 1048576
  59.8 28.1 %collective-permute-start.7 = (bf16[4,192,768]{2,1,0:T(8,128)(2,1)S(1)}, bf16[4,192,768]{2,1,0:T(8,128)(2,1)S(1)}, u32[]{:S(2)}, u32[]{:S(2)}) collective-permute-start(bf16[4,192,768]{2,1,0:T(8,128)(2,1)S(1)} %get-tuple-element.187), channel_id=1, source_target_pairs={{0,4},{1,5},{2,6},{3,7},{4,0},{5,1},{6,2},{7,3},{8,12},{9,13},{10,... | collective-permute-start | bytes 3538952 | tf_op jit(solution)/shard_map/ppermute | solution.py:627
  65.0 4.6 %collective-permute-start.6 = (bf16[8,48,3072]{2,1,0:T(8,128)(2,1)S(1)}, bf16[8,48,3072]{2,1,0:T(8,128)(2,1)S(1)}, u32[]{:S(2)}, u32[]{:S(2)}) collective-permute-start(bf16[8,48,3072]{2,1,0:T(8,128)(2,1)S(1)} %get-tuple-element.174), channel_id=1, source_target_pairs={{0,1},{1,0},{2,3},{3,2},{4,5},{5,4},{6,7},{7,6},{8,9},{9,8},{10,11... | collective-permute-start | bytes 7077896 | tf_op jit(solution)/shard_map/ppermute | solution.py:627
  70.2 28.1 %collective-permute-start.10 = (bf16[4,48,3072]{2,1,0:T(8,128)(2,1)S(1)}, bf16[4,48,3072]{2,1,0:T(8,128)(2,1)S(1)}, u32[]{:S(2)}, u32[]{:S(2)}) collective-permute-start(bf16[4,48,3072]{2,1,0:T(8,128)(2,1)S(1)} %get-tuple-element.209), channel_id=1, source_target_pairs={{0,2},{1,3},{2,0},{3,1},{4,6},{5,7},{6,4},{7,5},{8,10},{9,11},{10,... | collective-permute-start | bytes 3538952 | tf_op jit(solution)/shard_map/ppermute | solution.py:627
  80.2 3.8 %collective-permute-start.8 = (bf16[8,48,2304]{2,1,0:T(8,128)(2,1)S(1)}, bf16[8,48,2304]{2,1,0:T(8,128)(2,1)S(1)}, u32[]{:S(2)}, u32[]{:S(2)}) collective-permute-start(bf16[8,48,2304]{2,1,0:T(8,128)(2,1)S(1)} %get-tuple-element.189), channel_id=1, source_target_pairs={{0,1},{1,0},{2,3},{3,2},{4,5},{5,4},{6,7},{7,6},{8,9},{9,8},{10,11... | collective-permute-start | bytes 5308424 | tf_op jit(solution)/shard_map/ppermute | solution.py:627
  87.9 4.8 %copy-start.15 = (bf16[1,768,2304]{2,1,0:T(8,128)(2,1)S(1)}, bf16[1,768,2304]{2,1,0:T(8,128)(2,1)}, u32[]{:S(2)}) copy-start(bf16[1,768,2304]{2,1,0:T(8,128)(2,1)} %param.21) | copy-start | bytes 10616836
  88.2 28.4 %collective-permute-start.12 = (bf16[2,192,768]{2,1,0:T(8,128)(2,1)S(1)}, bf16[2,192,768]{2,1,0:T(8,128)(2,1)S(1)}, u32[]{:S(2)}, u32[]{:S(2)}) collective-permute-start(bf16[2,192,768]{2,1,0:T(8,128)(2,1)S(1)} %get-tuple-element.212), channel_id=1, source_target_pairs={{0,8},{1,9},{2,10},{3,11},{4,12},{5,13},{6,14},{7,15},{8,0},{9,1},... | collective-permute-start | bytes 1769480 | tf_op jit(solution)/shard_map/ppermute | solution.py:627
  92.6 3.0 %collective-permute-start.9 = (bf16[8,48,896]{2,1,0:T(8,128)(2,1)S(1)}, bf16[8,48,896]{2,1,0:T(8,128)(2,1)S(1)}, u32[]{:S(2)}, u32[]{:S(2)}) collective-permute-start(bf16[8,48,896]{2,1,0:T(8,128)(2,1)S(1)} %get-tuple-element.204), channel_id=1, source_target_pairs={{0,1},{1,0},{2,3},{3,2},{4,5},{5,4},{6,7},{7,6},{8,9},{9,8},{10,11... | collective-permute-start | bytes 2064392 | tf_op jit(solution)/shard_map/ppermute | solution.py:627
  98.2 18.5 %collective-permute-start.11 = (bf16[2,48,2304]{2,1,0:T(8,128)(2,1)S(1)}, bf16[2,48,2304]{2,1,0:T(8,128)(2,1)S(1)}, u32[]{:S(2)}, u32[]{:S(2)}) collective-permute-start(bf16[2,48,2304]{2,1,0:T(8,128)(2,1)S(1)} %get-tuple-element.210), channel_id=1, source_target_pairs={{0,2},{1,3},{2,0},{3,1},{4,6},{5,7},{6,4},{7,5},{8,10},{9,11},{10,... | collective-permute-start | bytes 1327112 | tf_op jit(solution)/shard_map/ppermute | solution.py:627
  99.2 19.9 %collective-permute-start.13 = (bf16[2,48,2304]{2,1,0:T(8,128)(2,1)S(1)}, bf16[2,48,2304]{2,1,0:T(8,128)(2,1)S(1)}, u32[]{:S(2)}, u32[]{:S(2)}) collective-permute-start(bf16[2,48,2304]{2,1,0:T(8,128)(2,1)S(1)} %get-tuple-element.220), channel_id=1, source_target_pairs={{0,2},{1,3},{2,0},{3,1},{4,6},{5,7},{6,4},{7,5},{8,10},{9,11},{10,... | collective-permute-start | bytes 1327112 | tf_op jit(solution)/shard_map/ppermute | solution.py:627
  100.5 22.4 %collective-permute-start.17 = (bf16[1,48,3072]{2,1,0:T(8,128)(2,1)S(1)}, bf16[1,48,3072]{2,1,0:T(8,128)(2,1)S(1)}, u32[]{:S(2)}, u32[]{:S(2)}) collective-permute-start(bf16[1,48,3072]{2,1,0:T(8,128)(2,1)S(1)} %get-tuple-element.232), channel_id=1, source_target_pairs={{0,4},{1,5},{2,6},{3,7},{4,0},{5,1},{6,2},{7,3},{8,12},{9,13},{10,... | collective-permute-start | bytes 884744 | tf_op jit(solution)/shard_map/ppermute | solution.py:627
  101.9 28.6 %collective-permute-start.16 = (bf16[1,48,3072]{2,1,0:T(8,128)(2,1)S(1)}, bf16[1,48,3072]{2,1,0:T(8,128)(2,1)S(1)}, u32[]{:S(2)}, u32[]{:S(2)}) collective-permute-start(bf16[1,48,3072]{2,1,0:T(8,128)(2,1)S(1)} %get-tuple-element.229), channel_id=1, source_target_pairs={{0,4},{1,5},{2,6},{3,7},{4,0},{5,1},{6,2},{7,3},{8,12},{9,13},{10,... | collective-permute-start | bytes 884744 | tf_op jit(solution)/shard_map/ppermute | solution.py:627
  119.1 11.6 %collective-permute-start.15 = (bf16[4,48,896]{2,1,0:T(8,128)(2,1)S(1)}, bf16[4,48,896]{2,1,0:T(8,128)(2,1)S(1)}, u32[]{:S(2)}, u32[]{:S(2)}) collective-permute-start(bf16[4,48,896]{2,1,0:T(8,128)(2,1)S(1)} %get-tuple-element.227), channel_id=1, source_target_pairs={{0,2},{1,3},{2,0},{3,1},{4,6},{5,7},{6,4},{7,5},{8,10},{9,11},{10,... | collective-permute-start | bytes 1032200 | tf_op jit(solution)/shard_map/ppermute | solution.py:627
  120.2 18.5 %collective-permute-start.18 = (bf16[1,48,2304]{2,1,0:T(8,128)(2,1)S(1)}, bf16[1,48,2304]{2,1,0:T(8,128)(2,1)S(1)}, u32[]{:S(2)}, u32[]{:S(2)}) collective-permute-start(bf16[1,48,2304]{2,1,0:T(8,128)(2,1)S(1)} %get-tuple-element.239), channel_id=1, source_target_pairs={{0,4},{1,5},{2,6},{3,7},{4,0},{5,1},{6,2},{7,3},{8,12},{9,13},{10,... | collective-permute-start | bytes 663560 | tf_op jit(solution)/shard_map/ppermute | solution.py:627
  121.6 23.3 %collective-permute-start.14 = (bf16[1,48,2304]{2,1,0:T(8,128)(2,1)S(1)}, bf16[1,48,2304]{2,1,0:T(8,128)(2,1)S(1)}, u32[]{:S(2)}, u32[]{:S(2)}) collective-permute-start(bf16[1,48,2304]{2,1,0:T(8,128)(2,1)S(1)} %get-tuple-element.224), channel_id=1, source_target_pairs={{0,4},{1,5},{2,6},{3,7},{4,0},{5,1},{6,2},{7,3},{8,12},{9,13},{10,... | collective-permute-start | bytes 663560 | tf_op jit(solution)/shard_map/ppermute | solution.py:627
  130.6 14.4 %collective-permute-start.22 = (bf16[1,48,3072]{2,1,0:T(8,128)(2,1)S(1)}, bf16[1,48,3072]{2,1,0:T(8,128)(2,1)S(1)}, u32[]{:S(2)}, u32[]{:S(2)}) collective-permute-start(bf16[1,48,3072]{2,1,0:T(8,128)(2,1)S(1)} %get-tuple-element.250), channel_id=1, source_target_pairs={{0,8},{1,9},{2,10},{3,11},{4,12},{5,13},{6,14},{7,15},{8,0},{9,1},... | collective-permute-start | bytes 884744 | tf_op jit(solution)/shard_map/ppermute | solution.py:627
  130.7 18.9 %collective-permute-start.20 = (bf16[1,192,768]{2,1,0:T(8,128)(2,1)S(1)}, bf16[1,192,768]{2,1,0:T(8,128)(2,1)S(1)}, u32[]{:S(2)}, u32[]{:S(2)}) collective-permute-start(bf16[1,192,768]{2,1,0:T(8,128)(2,1)S(1)} %get-tuple-element.246), channel_id=1, source_target_pairs={{0,2},{1,3},{2,0},{3,1},{4,6},{5,7},{6,4},{7,5},{8,10},{9,11},{10,... | collective-permute-start | bytes 884744 | tf_op jit(solution)/shard_map/ppermute | solution.py:627
  132.0 17.0 %collective-permute-start.21 = (bf16[2,48,896]{2,1,0:T(8,128)(2,1)S(1)}, bf16[2,48,896]{2,1,0:T(8,128)(2,1)S(1)}, u32[]{:S(2)}, u32[]{:S(2)}) collective-permute-start(bf16[2,48,896]{2,1,0:T(8,128)(2,1)S(1)} %get-tuple-element.248), channel_id=1, source_target_pairs={{0,4},{1,5},{2,6},{3,7},{4,0},{5,1},{6,2},{7,3},{8,12},{9,13},{10,... | collective-permute-start | bytes 516104 | tf_op jit(solution)/shard_map/ppermute | solution.py:627
  145.0 11.1 %collective-permute-start.19 = (bf16[1,48,2304]{2,1,0:T(8,128)(2,1)S(1)}, bf16[1,48,2304]{2,1,0:T(8,128)(2,1)S(1)}, u32[]{:S(2)}, u32[]{:S(2)}) collective-permute-start(bf16[1,48,2304]{2,1,0:T(8,128)(2,1)S(1)} %get-tuple-element.243), channel_id=1, source_target_pairs={{0,8},{1,9},{2,10},{3,11},{4,12},{5,13},{6,14},{7,15},{8,0},{9,1},... | collective-permute-start | bytes 663560 | tf_op jit(solution)/shard_map/ppermute | solution.py:627
  149.0 8.0 %collective-permute-start.23 = (bf16[1,48,896]{2,1,0:T(8,128)(2,1)S(1)}, bf16[1,48,896]{2,1,0:T(8,128)(2,1)S(1)}, u32[]{:S(2)}, u32[]{:S(2)}) collective-permute-start(bf16[1,48,896]{2,1,0:T(8,128)(2,1)S(1)} %get-tuple-element.257), channel_id=1, source_target_pairs={{0,8},{1,9},{2,10},{3,11},{4,12},{5,13},{6,14},{7,15},{8,0},{9,1},... | collective-permute-start | bytes 258056 | tf_op jit(solution)/shard_map/ppermute | solution.py:627

commit v2 on v1

--- a/solution.py
+++ b/solution.py
@@ -283,6 +283,12 @@
     )
     rest = jnp.zeros((PACKET - count - SEGS - 1, width), F32)
     out[...] = jnp.concatenate([q_rows, p_rows, row, rest], 0).astype(BF)
+
+
+def times_low(value, low):
+    rows = value.shape[0]
+    parts = nn(split_three(value), low)
+    return parts[:rows] + parts[rows : 2 * rows] + parts[2 * rows :]
 
 
 def loss_kernel(place, near, far, grad, *, order, count):
@@ -309,17 +315,12 @@
     soft = soft / jnp.sum(soft, -1, keepdims=True)
     grad_logits = soft - (number == label).astype(F32)
     grad_logits = grad_logits * (part < count).astype(F32)
-    wide = packets.astype(F32)
-    grad_q = jnp.dot(
-        grad_logits[:count], wide, precision=lax.Precision.HIGHEST, preferred_element_type=F32
-    )
+    grad_q = times_low(grad_logits[:count], packets)
     pick = lax.broadcasted_iota(jnp.int32, (count, 1), 0)
-    pick = jnp.logical_and(pick + count == col, pick < SEGS).astype(F32)
-    turned = lax.dot_general(
-        pick, grad_logits, (((1,), (1,)), ((), ())),
-        precision=lax.Precision.HIGHEST, preferred_element_type=F32,
-    )
-    grad_p = jnp.dot(turned, wide, precision=lax.Precision.HIGHEST, preferred_element_type=F32)
+    pick = jnp.logical_and(pick + count == col, pick < SEGS).astype(F32).astype(BF)
+    turned = nt(pick, split_three(grad_logits))
+    turned = turned[:, :total] + turned[:, total : 2 * total] + turned[:, 2 * total :]
+    grad_p = times_low(turned, packets)
     grad[...] = jnp.where(tower == 0, grad_q, grad_p) * scale
 
 

time: 158 us -> 157 us (level)
  transfers between devices with their start and end apart: 24 -> 24, of which waited for: 16 -> 16; matrix products, arithmetic and copies ran while one was open for 0% -> 0% of each run, Pallas kernels for 32% -> 33%
where the time goes in v2:
time: 157 us
  Pallas kernels  70.5 us (45%)
  waiting for transfers between devices  56.5 us (36%)
  starting transfers between devices  24 us (15%)
  local copies, waits for them, and re-layouts  4.44 us (3%)
    pallas_call x33, Pallas kernels, kernel_call(): pl.pallas_call(body, out_shape=shapes, in_specs=[SM] * smem + [VM] * (len...  70.5 us
    ppermute x24, waiting for transfers between devices, swapped(): return lax.ppermute(value, axis, [(i, i ^ mask) for i in range(count)])  56.5 us
    ppermute x24, starting transfers between devices, swapped(): return lax.ppermute(value, axis, [(i, i ^ mask) for i in range(count)])  24 us
    unnamed x44, local copies, waits for them, and re-layouts  4.29 us
  transfers between devices with their start and end apart: 24, of which 16 were waited for; matrix products, arithmetic and copies ran while one was open for 0% of the time, Pallas kernels for 33%

profile of v2, /device:TPU:0, one launch (start us, length us, event | category | flops | bytes accessed | tf_op | source)
XLA Modules:
  0.0 156.6 jit_solution(9988724628303371957)
XLA Ops:
  0.7 4.7 %proj.1 = bf16[512,2304]{1,0:T(8,128)(2,1)S(1)} custom-call(bf16[512,768]{1,0:T(8,128)(2,1)} %bitcast.23, bf16[768,2304]{1,0:T(8,128)(2,1)} %bitcast.39, f32[1,768]{1,0:T(1,128)} %bq_hbm.1, f32[1,768]{1,0:T(1,128)} %bv_hbm.1), custom_call_target="tpu_custom_call" | custom-call | flops 3000000000 | tf_op jit(solution)/shard_map/proj/pallas_call | solution.py:42
  6.1 1.3 copy-done.3
  7.3 4.6 %cls.1 = bf16[16,768]{1,0:T(8,128)(2,1)S(1)} custom-call(s32[2]{0:T(128)S(1)} %pad_add_fusion.place, s32[1,512]{1,0:T(1,128)S(1)} %copy-done.6, bf16[512,768]{1,0:T(8,128)(2,1)S(1)} %bitcast.24, bf16[512,2304]{1,0:T(8,128)(2,1)S(1)} %proj.1, bf16[768,768]{1,0:T(8,128)(2,1)S(1)} %bitcast.33, bf16[768,3072]{1,0:T(8,128)(2,1)S(1)} %bitcast.28, ...), custom_call_target="tpu_custom_call" | custom-call | flops 3000000000 | tf_op jit(solution)/shard_map/cls/pallas_call | solution.py:42
  11.9 3.0 %collective-permute-start = (bf16[16,768]{1,0:T(8,128)(2,1)S(1)}, bf16[16,768]{1,0:T(8,128)(2,1)S(1)}, u32[]{:S(2)}, u32[]{:S(2)}) collective-permute-start(bf16[16,768]{1,0:T(8,128)(2,1)S(1)} %cls.1), channel_id=1, source_target_pairs={{0,16},{16,0},{1,17},{17,1},{2,18},{18,2},{3,19},{19,3},{4,20},{20... | collective-permute-start | bytes 73736 | tf_op jit(solution)/shard_map/ppermute | solution.py:628
  15.2 7.0 %attention.1 = (bf16[512,768]{1,0:T(8,128)(2,1)S(1)}, bf16[12,512,512]{2,1,0:T(8,128)(2,1)S(1)}) custom-call(s32[2]{0:T(128)S(1)} %pad_add_fusion.place, s32[1,512]{1,0:T(1,128)S(1)} %copy-done.6, s32[512,1]{1,0:T(8,128)S(1)} %copy.32.seg_col, bf16[512,2304]{1,0:T(8,128)(2,1)S(1)} %proj.1), custom_call_target="tpu_custom_call" | custom-call | flops 8000000000 | tf_op jit(solution)/shard_map/attention/pallas_call | solution.py:42
  22.8 2.7 %collective-permute-start.1 = (bf16[24,768]{1,0:T(8,128)(2,1)S(1)}, bf16[24,768]{1,0:T(8,128)(2,1)S(1)}, u32[]{:S(2)}, u32[]{:S(2)}) collective-permute-start(bf16[24,768]{1,0:T(8,128)(2,1)S(1)} %packet.1), channel_id=1, source_target_pairs={{0,8},{1,9},{2,10},{3,11},{4,12},{5,13},{6,14},{7,15},{8,0},{9,1},... | collective-permute-start | bytes 110600 | tf_op jit(solution)/shard_map/ppermute | solution.py:628
  25.4 1.7 %first.1 = (f32[512,768]{1,0:T(8,128)S(1)}, f32[512,1]{1,0:T(8,128)S(1)}, bf16[512,768]{1,0:T(8,128)(2,1)S(1)}) custom-call(bf16[512,768]{1,0:T(8,128)(2,1)S(1)} %bitcast.25, bf16[512,768]{1,0:T(8,128)(2,1)S(1)} %get-tuple-element.145.attended.refs_2_, bf16[768,768]{1,0:T(8,128)(2,1)S(1)} %bitcast.34, f32[1,768]{1,0:T(1,128)S(1)} %copy-done.9, ...), custom_call_target="tpu_custom_call" | custom-call | flops 2000000000 | tf_op jit(solution)/shard_map/first/pallas_call | solution.py:42
  27.7 1.6 %collective-permute-start.2 = (bf16[48,768]{1,0:T(8,128)(2,1)S(1)}, bf16[48,768]{1,0:T(8,128)(2,1)S(1)}, u32[]{:S(2)}, u32[]{:S(2)}) collective-permute-start(bf16[48,768]{1,0:T(8,128)(2,1)S(1)} %pad_maximum_fusion.2), channel_id=1, source_target_pairs={{0,4},{1,5},{2,6},{3,7},{4,0},{5,1},{6,2},{7,3},{8,12},{9,13},{10,... | collective-permute-start | bytes 221192 | tf_op jit(solution)/shard_map/ppermute | solution.py:628
  29.4 2.3 %copy-done.2 = bf16[1,768,3072]{2,1,0:T(8,128)(2,1)S(1)} copy-done((bf16[1,768,3072]{2,1,0:T(8,128)(2,1)S(1)}, bf16[1,768,3072]{2,1,0:T(8,128)(2,1)}, u32[]{:S(2)}) %copy-start.2) | copy-done | bytes 4718616
  31.7 6.0 %inner.1 = (bf16[512,3072]{1,0:T(8,128)(2,1)S(1)}, bf16[512,3072]{1,0:T(8,128)(2,1)S(1)}) custom-call(bf16[512,768]{1,0:T(8,128)(2,1)S(1)} %get-tuple-element.148.low.refs_0_, bf16[768,3072]{1,0:T(8,128)(2,1)S(1)} %bitcast.29, f32[1,3072]{1,0:T(1,128)S(1)} %copy-done.8), custom_call_target="tpu_custom_call" | custom-call | flops 6000000000 | tf_op jit(solution)/shard_map/inner/pallas_call | solution.py:42
  37.7 1.6 collective-permute-start.3
  39.3 4.2 %second.1 = (f32[512,768]{1,0:T(8,128)S(1)}, f32[512,1]{1,0:T(8,128)S(1)}, bf16[512,768]{1,0:T(8,128)(2,1)}) custom-call(bf16[512,3072]{1,0:T(8,128)(2,1)S(1)} %get-tuple-element.151.act.refs_0_, bf16[3072,768]{1,0:T(8,128)(2,1)S(1)} %bitcast.21, f32[1,768]{1,0:T(1,128)S(1)} %copy-done.11, f32[512,768]{1,0:T(8,128)S(1)} %get-tuple-element.152.n1, ...), custom_call_target="tpu_custom_call" | custom-call | flops 4000000000 | tf_op jit(solution)/shard_map/second/pallas_call | solution.py:42
  43.6 1.6 %collective-permute-done.4.far = bf16[192,768]{1,0:T(8,128)(2,1)S(1)} collective-permute-done((bf16[192,768]{1,0:T(8,128)(2,1)S(1)}, bf16[192,768]{1,0:T(8,128)(2,1)S(1)}, u32[]{:S(2)}, u32[]{:S(2)}) %collective-permute-start.4) | collective-permute-done | bytes 294944 | tf_op jit(solution)/shard_map/ppermute | solution.py:628
  45.2 2.0 %loss.1.cls_grad = f32[16,768]{1,0:T(8,128)S(1)} custom-call(s32[2]{0:T(128)S(1)} %pad_add_fusion.place, bf16[192,768]{1,0:T(8,128)(2,1)S(1)} %pad_maximum_fusion.near, bf16[192,768]{1,0:T(8,128)(2,1)S(1)} %collective-permute-done.4.far), custom_call_target="tpu_custom_call" | custom-call | tf_op jit(solution)/shard_map/loss/pallas_call | solution.py:42
  47.1 1.9 %second_back.1 = (f32[512,768]{1,0:T(8,128)S(1)}, bf16[512,768]{1,0:T(8,128)(2,1)S(1)}, f32[8,768]{1,0:T(8,128)S(1)}) custom-call(s32[2]{0:T(128)S(1)} %pad_add_fusion.place, s32[1,512]{1,0:T(1,128)S(1)} %copy-done.6, bf16[512,768]{1,0:T(8,128)(2,1)S(1)} %bitcast.36, f32[16,768]{1,0:T(8,128)S(1)} %loss.1.cls_grad, f32[512,768]{1,0:T(8,128)S(1)} %get-tuple-element.156.n2, ...), custom_call_target="tpu_custom_call" | custom-call | tf_op jit(solution)/shard_map/second_back/pallas_call | solution.py:42
  49.1 4.3 %grad_w_back.1 = (bf16[8,192,768]{2,1,0:T(8,128)(2,1)S(1)}, bf16[8,192,768]{2,1,0:T(8,128)(2,1)S(1)}) custom-call(s32[2]{0:T(128)S(1)} %pad_add_fusion.place, bf16[512,3072]{1,0:T(8,128)(2,1)S(1)} %get-tuple-element.151.act.refs_0_, bf16[512,768]{1,0:T(8,128)(2,1)S(1)} %get-tuple-element.160.refs_1_.low), custom_call_target="tpu_custom_call" | custom-call | tf_op jit(solution)/shard_map/grad_w_back/pallas_call | solution.py:42
  53.6 3.5 %inner_back.1 = (bf16[512,3072]{1,0:T(8,128)(2,1)S(1)}, f32[1,3072]{1,0:T(1,128)S(1)}) custom-call(bf16[512,768]{1,0:T(8,128)(2,1)S(1)} %get-tuple-element.160.refs_1_.low, bf16[3072,768]{1,0:T(8,128)(2,1)S(1)} %bitcast.22, bf16[512,3072]{1,0:T(8,128)(2,1)S(1)} %get-tuple-element.161.slope), custom_call_target="tpu_custom_call" | custom-call | tf_op jit(solution)/shard_map/inner_back/pallas_call | solution.py:42
  57.1 0.9 collective-permute-done.5.refs_1_
  59.3 4.4 %grad_w_in.1 = (bf16[8,48,3072]{2,1,0:T(8,128)(2,1)S(1)}, bf16[8,48,3072]{2,1,0:T(8,128)(2,1)S(1)}) custom-call(s32[2]{0:T(128)S(1)} %pad_add_fusion.place, bf16[512,768]{1,0:T(8,128)(2,1)S(1)} %get-tuple-element.148.low.refs_0_, bf16[512,3072]{1,0:T(8,128)(2,1)S(1)} %get-tuple-element.169.refs_1_.inner), custom_call_target="tpu_custom_call" | custom-call | tf_op jit(solution)/shard_map/grad_w_in/pallas_call | solution.py:42
  63.8 4.0 %first_back.1 = (f32[512,768]{1,0:T(8,128)S(1)}, bf16[512,768]{1,0:T(8,128)(2,1)S(1)}, bf16[512,768]{1,0:T(8,128)(2,1)S(1)}, f32[8,768]{1,0:T(8,128)S(1)}) custom-call(bf16[512,3072]{1,0:T(8,128)(2,1)S(1)} %get-tuple-element.169.refs_1_.inner, bf16[768,3072]{1,0:T(8,128)(2,1)S(1)} %bitcast.32, f32[512,768]{1,0:T(8,128)S(1)} %get-tuple-element.170.grad_second, ...), custom_call_target="tpu_custom_call" | custom-call | flops 30000001024 | tf_op jit(solution)/shard_map/first_back/pallas_call | solution.py:42
  68.9 1.0 collective-permute-start.10
  69.9 5.6 %attention_back_0.1 = (bf16[512,1536]{1,0:T(8,128)(2,1)S(1)}, f32[1,1536]{1,0:T(1,128)S(1)}) custom-call(bf16[512,2304]{1,0:T(8,128)(2,1)S(1)} %proj.1, bf16[12,512,512]{2,1,0:T(8,128)(2,1)S(1)} %get-tuple-element.154.probs, bf16[512,768]{1,0:T(8,128)(2,1)S(1)} %get-tuple-element.184.att_grad), custom_call_target="tpu_custom_call" | custom-call | tf_op jit(solution)/shard_map/attention_back_0/pallas_call | solution.py:42
  75.4 3.5 %grad_w_qkv_1.1 = (bf16[8,48,2304]{2,1,0:T(8,128)(2,1)S(1)}, bf16[8,48,2304]{2,1,0:T(8,128)(2,1)S(1)}) custom-call(s32[2]{0:T(128)S(1)} %pad_add_fusion.place, bf16[512,768]{1,0:T(8,128)(2,1)S(1)} %bitcast.26, bf16[512,1536]{1,0:T(8,128)(2,1)S(1)} %get-tuple-element.180.refs_1_.left, bf16[512,768]{1,0:T(8,128)(2,1)S(1)} %get-tuple-element.145.attended.refs_2_, ...), custom_call_target="tpu_custom_call" | custom-call | tf_op jit(solution)/shard_map/grad_w_qkv_1/pallas_call | solution.py:42
  79.0 2.7 %attention_back_4.1 = (bf16[512,768]{1,0:T(8,128)(2,1)S(1)}, f32[1,768]{1,0:T(1,128)S(1)}) custom-call(bf16[512,2304]{1,0:T(8,128)(2,1)S(1)} %proj.1, bf16[12,512,512]{2,1,0:T(8,128)(2,1)S(1)} %get-tuple-element.154.probs, bf16[512,768]{1,0:T(8,128)(2,1)S(1)} %get-tuple-element.184.att_grad), custom_call_target="tpu_custom_call" | custom-call | flops 30000001024 | tf_op jit(solution)/shard_map/attention_back_4/pallas_call | solution.py:42
  81.7 1.0 collective-permute-done.8.refs_1_
  83.1 3.5 %collective-permute-done.7.refs_1_ = bf16[4,192,768]{2,1,0:T(8,128)(2,1)S(1)} collective-permute-done((bf16[4,192,768]{2,1,0:T(8,128)(2,1)S(1)}, bf16[4,192,768]{2,1,0:T(8,128)(2,1)S(1)}, u32[]{:S(2)}, u32[]{:S(2)}) %collective-permute-start.7) | collective-permute-done | bytes 1179680 | tf_op jit(solution)/shard_map/ppermute | solution.py:628
  86.9 2.9 %collective-permute-start.12 = (bf16[2,192,768]{2,1,0:T(8,128)(2,1)S(1)}, bf16[2,192,768]{2,1,0:T(8,128)(2,1)S(1)}, u32[]{:S(2)}, u32[]{:S(2)}) collective-permute-start(bf16[2,192,768]{2,1,0:T(8,128)(2,1)S(1)} %get-tuple-element.212), channel_id=1, source_target_pairs={{0,8},{1,9},{2,10},{3,11},{4,12},{5,13},{6,14},{7,15},{8,0},{9,1},... | collective-permute-start | bytes 1769480 | tf_op jit(solution)/shard_map/ppermute | solution.py:628
  89.8 1.5 grad_w_qkv_2.1
  91.4 2.9 %input_back.1 = bf16[512,768]{1,0:T(8,128)(2,1)} custom-call(bf16[512,1536]{1,0:T(8,128)(2,1)S(1)} %get-tuple-element.180.refs_1_.left, bf16[512,768]{1,0:T(8,128)(2,1)S(1)} %get-tuple-element.201.grad_proj.right, bf16[768,2304]{1,0:T(8,128)(2,1)S(1)} %bitcast.40, f32[512,768]{1,0:T(8,128)S(1)} %get-tuple-element.175.grad_first), custom_call_target="tpu_custom_call" | custom-call | flops 30000001024 | tf_op jit(solution)/shard_map/input_back/pallas_call | solution.py:42
  94.5 2.5 %collective-permute-done.10.refs_1_ = bf16[4,48,3072]{2,1,0:T(8,128)(2,1)S(1)} collective-permute-done((bf16[4,48,3072]{2,1,0:T(8,128)(2,1)S(1)}, bf16[4,48,3072]{2,1,0:T(8,128)(2,1)S(1)}, u32[]{:S(2)}, u32[]{:S(2)}) %collective-permute-start.10) | collective-permute-done | bytes 1179680 | tf_op jit(solution)/shard_map/ppermute | solution.py:628
  96.9 0.9 collective-permute-start.11
  97.9 1.1 collective-permute-start.13
  99.2 1.4 collective-permute-start.17
  101.3 14.0 %collective-permute-done.12.refs_1_ = bf16[2,192,768]{2,1,0:T(8,128)(2,1)S(1)} collective-permute-done((bf16[2,192,768]{2,1,0:T(8,128)(2,1)S(1)}, bf16[2,192,768]{2,1,0:T(8,128)(2,1)S(1)}, u32[]{:S(2)}, u32[]{:S(2)}) %collective-permute-start.12) | collective-permute-done | bytes 589856 | tf_op jit(solution)/shard_map/ppermute | solution.py:628
  115.5 2.4 %collective-permute-done.13.refs_2_ = bf16[2,48,2304]{2,1,0:T(8,128)(2,1)S(1)} collective-permute-done((bf16[2,48,2304]{2,1,0:T(8,128)(2,1)S(1)}, bf16[2,48,2304]{2,1,0:T(8,128)(2,1)S(1)}, u32[]{:S(2)}, u32[]{:S(2)}) %collective-permute-start.13) | collective-permute-done | bytes 442400 | tf_op jit(solution)/shard_map/ppermute | solution.py:628
  117.8 0.9 collective-permute-start.15
  118.9 1.4 collective-permute-start.18
  121.7 7.5 %collective-permute-done.16.refs_1_ = bf16[1,48,3072]{2,1,0:T(8,128)(2,1)S(1)} collective-permute-done((bf16[1,48,3072]{2,1,0:T(8,128)(2,1)S(1)}, bf16[1,48,3072]{2,1,0:T(8,128)(2,1)S(1)}, u32[]{:S(2)}, u32[]{:S(2)}) %collective-permute-start.16) | collective-permute-done | bytes 294944 | tf_op jit(solution)/shard_map/ppermute | solution.py:628
  129.5 1.2 collective-permute-start.20
  130.7 0.8 collective-permute-start.21
  131.5 5.9 %collective-permute-done.18.refs_2_ = bf16[1,48,2304]{2,1,0:T(8,128)(2,1)S(1)} collective-permute-done((bf16[1,48,2304]{2,1,0:T(8,128)(2,1)S(1)}, bf16[1,48,2304]{2,1,0:T(8,128)(2,1)S(1)}, u32[]{:S(2)}, u32[]{:S(2)}) %collective-permute-start.18) | collective-permute-done | bytes 221216 | tf_op jit(solution)/shard_map/ppermute | solution.py:628
  137.4 6.1 %collective-permute-done.14.refs_1_ = bf16[1,48,2304]{2,1,0:T(8,128)(2,1)S(1)} collective-permute-done((bf16[1,48,2304]{2,1,0:T(8,128)(2,1)S(1)}, bf16[1,48,2304]{2,1,0:T(8,128)(2,1)S(1)}, u32[]{:S(2)}, u32[]{:S(2)}) %collective-permute-start.14) | collective-permute-done | bytes 221216 | tf_op jit(solution)/shard_map/ppermute | solution.py:628
  143.8 0.9 finish.2
  144.6 3.0 %collective-permute-done.21.refs_1_ = bf16[2,48,896]{2,1,0:T(8,128)(2,1)S(1)} collective-permute-done((bf16[2,48,896]{2,1,0:T(8,128)(2,1)S(1)}, bf16[2,48,896]{2,1,0:T(8,128)(2,1)S(1)}, u32[]{:S(2)}, u32[]{:S(2)}) %collective-permute-start.21) | collective-permute-done | bytes 172064 | tf_op jit(solution)/shard_map/ppermute | solution.py:628
  148.3 0.9 finish.3
  149.2 5.6 %collective-permute-done.19.came = bf16[1,48,2304]{2,1,0:T(8,128)(2,1)S(1)} collective-permute-done((bf16[1,48,2304]{2,1,0:T(8,128)(2,1)S(1)}, bf16[1,48,2304]{2,1,0:T(8,128)(2,1)S(1)}, u32[]{:S(2)}, u32[]{:S(2)}) %collective-permute-start.19) | collective-permute-done | bytes 221216 | tf_op jit(solution)/shard_map/ppermute | solution.py:628
  154.8 0.9 collective-permute-done.23.came_last
  155.7 0.9 finish_last.1
  (85 shorter events, 9.5 us)
Async XLA Ops:
  0.7 4.7 %slice-start = ((s8[4718592]{0:T(1024)(128)(4,1)}), s8[4194304]{0:T(1024)(128)(4,1)S(1)}, s32[]{:S(2)}) async-start(s8[4718592]{0:T(1024)(128)(4,1)} %bitcast.16), calls=%async_computation | async-start | bytes 8388608
  0.7 4.7 %slice-start.1 = ((s8[4718592]{0:T(1024)(128)(4,1)}), s8[524288]{0:T(1024)(128)(4,1)S(1)}, s32[]{:S(2)}) async-start(s8[4718592]{0:T(1024)(128)(4,1)} %bitcast.16), calls=%async_computation.1 | async-start | bytes 1048576
  0.7 4.7 %copy-start = (bf16[1,512,768]{2,1,0:T(8,128)(2,1)S(1)}, bf16[1,512,768]{2,1,0:T(8,128)(2,1)}, u32[]{:S(2)}) copy-start(bf16[1,512,768]{2,1,0:T(8,128)(2,1)} %param.17) | copy-start | bytes 2359300
  0.7 5.3 %copy-start.1 = (bf16[1,768,3072]{2,1,0:T(8,128)(2,1)S(1)}, bf16[1,768,3072]{2,1,0:T(8,128)(2,1)}, u32[]{:S(2)}) copy-start(bf16[1,768,3072]{2,1,0:T(8,128)(2,1)} %param.28) | copy-start | bytes 14155780
  0.7 5.3 %copy-start.6 = (s32[1,512]{1,0:T(1,128)S(1)}, s32[1,512]{1,0:T(1,128)}, u32[]{:S(2)}) copy-start(s32[1,512]{1,0:T(1,128)} %seg.3) | copy-start | bytes 6148
  6.1 1.3 copy-start.3
  11.9 10.3 %collective-permute-start = (bf16[16,768]{1,0:T(8,128)(2,1)S(1)}, bf16[16,768]{1,0:T(8,128)(2,1)S(1)}, u32[]{:S(2)}, u32[]{:S(2)}) collective-permute-start(bf16[16,768]{1,0:T(8,128)(2,1)S(1)} %cls.1), channel_id=1, source_target_pairs={{0,16},{16,0},{1,17},{17,1},{2,18},{18,2},{3,19},{19,3},{4,20},{20... | collective-permute-start | bytes 73736 | tf_op jit(solution)/shard_map/ppermute | solution.py:628
  15.1 7.1 %copy-start.14 = (s32[16]{0:T(128)S(1)}, s32[16]{0:T(128)}, u32[]{:S(2)}) copy-start(s32[16]{0:T(128)} %param.19) | copy-start | bytes 196
  15.1 10.3 %copy-start.4 = (bf16[1,768,768]{2,1,0:T(8,128)(2,1)S(1)}, bf16[1,768,768]{2,1,0:T(8,128)(2,1)}, u32[]{:S(2)}) copy-start(bf16[1,768,768]{2,1,0:T(8,128)(2,1)} %param.24) | copy-start | bytes 3538948
  15.1 10.3 %copy-start.9 = (f32[1,768]{1,0:T(1,128)S(1)}, f32[1,768]{1,0:T(1,128)}, u32[]{:S(2)}) copy-start(f32[1,768]{1,0:T(1,128)} %b_out.1) | copy-start | bytes 9220
  15.1 10.3 %copy-start.10 = (f32[1,768]{1,0:T(1,128)S(1)}, f32[1,768]{1,0:T(1,128)}, u32[]{:S(2)}) copy-start(f32[1,768]{1,0:T(1,128)} %b1.3) | copy-start | bytes 9220
  15.1 10.3 %copy-start.13 = (f32[1,768]{1,0:T(1,128)S(1)}, f32[1,768]{1,0:T(1,128)}, u32[]{:S(2)}) copy-start(f32[1,768]{1,0:T(1,128)} %g1.5) | copy-start | bytes 9220
  22.7 6.6 %copy-start.8 = (f32[1,3072]{1,0:T(1,128)S(1)}, f32[1,3072]{1,0:T(1,128)}, u32[]{:S(2)}) copy-start(f32[1,3072]{1,0:T(1,128)} %b_in.1) | copy-start | bytes 36868
  22.8 4.9 %collective-permute-start.1 = (bf16[24,768]{1,0:T(8,128)(2,1)S(1)}, bf16[24,768]{1,0:T(8,128)(2,1)S(1)}, u32[]{:S(2)}, u32[]{:S(2)}) collective-permute-start(bf16[24,768]{1,0:T(8,128)(2,1)S(1)} %packet.1), channel_id=1, source_target_pairs={{0,8},{1,9},{2,10},{3,11},{4,12},{5,13},{6,14},{7,15},{8,0},{9,1},... | collective-permute-start | bytes 110600 | tf_op jit(solution)/shard_map/ppermute | solution.py:628
  27.7 11.6 %slice-start.2 = ((s8[4718592]{0:T(1024)(128)(4,1)}), s8[4194304]{0:T(1024)(128)(4,1)S(1)}, s32[]{:S(2)}) async-start(s8[4718592]{0:T(1024)(128)(4,1)} %bitcast.19), calls=%async_computation.2 | async-start | bytes 8388608
  27.7 11.6 %slice-start.3 = ((s8[4718592]{0:T(1024)(128)(4,1)}), s8[524288]{0:T(1024)(128)(4,1)S(1)}, s32[]{:S(2)}) async-start(s8[4718592]{0:T(1024)(128)(4,1)} %bitcast.19), calls=%async_computation.3 | async-start | bytes 1048576
  27.7 10.0 %collective-permute-start.2 = (bf16[48,768]{1,0:T(8,128)(2,1)S(1)}, bf16[48,768]{1,0:T(8,128)(2,1)S(1)}, u32[]{:S(2)}, u32[]{:S(2)}) collective-permute-start(bf16[48,768]{1,0:T(8,128)(2,1)S(1)} %pad_maximum_fusion.2), channel_id=1, source_target_pairs={{0,4},{1,5},{2,6},{3,7},{4,0},{5,1},{6,2},{7,3},{8,12},{9,13},{10,... | collective-permute-start | bytes 221192 | tf_op jit(solution)/shard_map/ppermute | solution.py:628
  29.4 2.3 %copy-start.2 = (bf16[1,768,3072]{2,1,0:T(8,128)(2,1)S(1)}, bf16[1,768,3072]{2,1,0:T(8,128)(2,1)}, u32[]{:S(2)}) copy-start(bf16[1,768,3072]{2,1,0:T(8,128)(2,1)} %param.28) | copy-start | bytes 14155780
  31.7 7.6 %copy-start.7 = (f32[1,768]{1,0:T(1,128)S(1)}, f32[1,768]{1,0:T(1,128)}, u32[]{:S(2)}) copy-start(f32[1,768]{1,0:T(1,128)} %g2.3) | copy-start | bytes 9220
  31.7 7.6 %copy-start.11 = (f32[1,768]{1,0:T(1,128)S(1)}, f32[1,768]{1,0:T(1,128)}, u32[]{:S(2)}) copy-start(f32[1,768]{1,0:T(1,128)} %b_back.1) | copy-start | bytes 9220
  31.7 7.6 %copy-start.12 = (f32[1,768]{1,0:T(1,128)S(1)}, f32[1,768]{1,0:T(1,128)}, u32[]{:S(2)}) copy-start(f32[1,768]{1,0:T(1,128)} %b2.1) | copy-start | bytes 9220
  37.7 5.8 %collective-permute-start.3 = (bf16[96,768]{1,0:T(8,128)(2,1)S(1)}, bf16[96,768]{1,0:T(8,128)(2,1)S(1)}, u32[]{:S(2)}, u32[]{:S(2)}) collective-permute-start(bf16[96,768]{1,0:T(8,128)(2,1)S(1)} %pad_maximum_fusion.1), channel_id=1, source_target_pairs={{0,2},{1,3},{2,0},{3,1},{4,6},{5,7},{6,4},{7,5},{8,10},{9,11},{10,... | collective-permute-start | bytes 442376 | tf_op jit(solution)/shard_map/ppermute | solution.py:628
  43.5 3.7 %copy-start.5 = (bf16[1,512,768]{2,1,0:T(8,128)(2,1)S(1)}, bf16[1,512,768]{2,1,0:T(8,128)(2,1)}, u32[]{:S(2)}) copy-start(bf16[1,512,768]{2,1,0:T(8,128)(2,1)} %param.20) | copy-start | bytes 2359300
  43.5 1.6 %collective-permute-start.4 = (bf16[192,768]{1,0:T(8,128)(2,1)S(1)}, bf16[192,768]{1,0:T(8,128)(2,1)S(1)}, u32[]{:S(2)}, u32[]{:S(2)}) collective-permute-start(bf16[192,768]{1,0:T(8,128)(2,1)S(1)} %pad_maximum_fusion.near), channel_id=1, source_target_pairs={{0,1},{1,0},{2,3},{3,2},{4,5},{5,4},{6,7},{7,6},{8,9},{9,8},{10,11... | collective-permute-start | bytes 884744 | tf_op jit(solution)/shard_map/ppermute | solution.py:628
  53.4 4.6 %collective-permute-start.5 = (bf16[8,192,768]{2,1,0:T(8,128)(2,1)S(1)}, bf16[8,192,768]{2,1,0:T(8,128)(2,1)S(1)}, u32[]{:S(2)}, u32[]{:S(2)}) collective-permute-start(bf16[8,192,768]{2,1,0:T(8,128)(2,1)S(1)} %get-tuple-element.164), channel_id=1, source_target_pairs={{0,1},{1,0},{2,3},{3,2},{4,5},{5,4},{6,7},{7,6},{8,9},{9,8},{10,11... | collective-permute-start | bytes 7077896 | tf_op jit(solution)/shard_map/ppermute | solution.py:628
  53.6 10.2 %slice-start.4 = ((s8[4718592]{0:T(1024)(128)(4,1)}), s8[4194304]{0:T(1024)(128)(4,1)S(1)}, s32[]{:S(2)}) async-start(s8[4718592]{0:T(1024)(128)(4,1)} %bitcast.30), calls=%async_computation.4 | async-start | bytes 8388608
  58.0 5.8 %slice-start.5 = ((s8[4718592]{0:T(1024)(128)(4,1)}), s8[524288]{0:T(1024)(128)(4,1)S(1)}, s32[]{:S(2)}) async-start(s8[4718592]{0:T(1024)(128)(4,1)} %bitcast.30), calls=%async_computation.5 | async-start | bytes 1048576
  58.5 28.1 %collective-permute-start.7 = (bf16[4,192,768]{2,1,0:T(8,128)(2,1)S(1)}, bf16[4,192,768]{2,1,0:T(8,128)(2,1)S(1)}, u32[]{:S(2)}, u32[]{:S(2)}) collective-permute-start(bf16[4,192,768]{2,1,0:T(8,128)(2,1)S(1)} %get-tuple-element.187), channel_id=1, source_target_pairs={{0,4},{1,5},{2,6},{3,7},{4,0},{5,1},{6,2},{7,3},{8,12},{9,13},{10,... | collective-permute-start | bytes 3538952 | tf_op jit(solution)/shard_map/ppermute | solution.py:628
  63.7 4.6 %collective-permute-start.6 = (bf16[8,48,3072]{2,1,0:T(8,128)(2,1)S(1)}, bf16[8,48,3072]{2,1,0:T(8,128)(2,1)S(1)}, u32[]{:S(2)}, u32[]{:S(2)}) collective-permute-start(bf16[8,48,3072]{2,1,0:T(8,128)(2,1)S(1)} %get-tuple-element.174), channel_id=1, source_target_pairs={{0,1},{1,0},{2,3},{3,2},{4,5},{5,4},{6,7},{7,6},{8,9},{9,8},{10,11... | collective-permute-start | bytes 7077896 | tf_op jit(solution)/shard_map/ppermute | solution.py:628
  68.9 28.1 %collective-permute-start.10 = (bf16[4,48,3072]{2,1,0:T(8,128)(2,1)S(1)}, bf16[4,48,3072]{2,1,0:T(8,128)(2,1)S(1)}, u32[]{:S(2)}, u32[]{:S(2)}) collective-permute-start(bf16[4,48,3072]{2,1,0:T(8,128)(2,1)S(1)} %get-tuple-element.209), channel_id=1, source_target_pairs={{0,2},{1,3},{2,0},{3,1},{4,6},{5,7},{6,4},{7,5},{8,10},{9,11},{10,... | collective-permute-start | bytes 3538952 | tf_op jit(solution)/shard_map/ppermute | solution.py:628
  78.9 3.8 %collective-permute-start.8 = (bf16[8,48,2304]{2,1,0:T(8,128)(2,1)S(1)}, bf16[8,48,2304]{2,1,0:T(8,128)(2,1)S(1)}, u32[]{:S(2)}, u32[]{:S(2)}) collective-permute-start(bf16[8,48,2304]{2,1,0:T(8,128)(2,1)S(1)} %get-tuple-element.189), channel_id=1, source_target_pairs={{0,1},{1,0},{2,3},{3,2},{4,5},{5,4},{6,7},{7,6},{8,9},{9,8},{10,11... | collective-permute-start | bytes 5308424 | tf_op jit(solution)/shard_map/ppermute | solution.py:628
  86.6 4.8 %copy-start.15 = (bf16[1,768,2304]{2,1,0:T(8,128)(2,1)S(1)}, bf16[1,768,2304]{2,1,0:T(8,128)(2,1)}, u32[]{:S(2)}) copy-start(bf16[1,768,2304]{2,1,0:T(8,128)(2,1)} %param.21) | copy-start | bytes 10616836
  86.9 28.4 %collective-permute-start.12 = (bf16[2,192,768]{2,1,0:T(8,128)(2,1)S(1)}, bf16[2,192,768]{2,1,0:T(8,128)(2,1)S(1)}, u32[]{:S(2)}, u32[]{:S(2)}) collective-permute-start(bf16[2,192,768]{2,1,0:T(8,128)(2,1)S(1)} %get-tuple-element.212), channel_id=1, source_target_pairs={{0,8},{1,9},{2,10},{3,11},{4,12},{5,13},{6,14},{7,15},{8,0},{9,1},... | collective-permute-start | bytes 1769480 | tf_op jit(solution)/shard_map/ppermute | solution.py:628
  91.3 3.0 %collective-permute-start.9 = (bf16[8,48,896]{2,1,0:T(8,128)(2,1)S(1)}, bf16[8,48,896]{2,1,0:T(8,128)(2,1)S(1)}, u32[]{:S(2)}, u32[]{:S(2)}) collective-permute-start(bf16[8,48,896]{2,1,0:T(8,128)(2,1)S(1)} %get-tuple-element.204), channel_id=1, source_target_pairs={{0,1},{1,0},{2,3},{3,2},{4,5},{5,4},{6,7},{7,6},{8,9},{9,8},{10,11... | collective-permute-start | bytes 2064392 | tf_op jit(solution)/shard_map/ppermute | solution.py:628
  96.9 18.5 %collective-permute-start.11 = (bf16[2,48,2304]{2,1,0:T(8,128)(2,1)S(1)}, bf16[2,48,2304]{2,1,0:T(8,128)(2,1)S(1)}, u32[]{:S(2)}, u32[]{:S(2)}) collective-permute-start(bf16[2,48,2304]{2,1,0:T(8,128)(2,1)S(1)} %get-tuple-element.210), channel_id=1, source_target_pairs={{0,2},{1,3},{2,0},{3,1},{4,6},{5,7},{6,4},{7,5},{8,10},{9,11},{10,... | collective-permute-start | bytes 1327112 | tf_op jit(solution)/shard_map/ppermute | solution.py:628
  97.9 19.9 %collective-permute-start.13 = (bf16[2,48,2304]{2,1,0:T(8,128)(2,1)S(1)}, bf16[2,48,2304]{2,1,0:T(8,128)(2,1)S(1)}, u32[]{:S(2)}, u32[]{:S(2)}) collective-permute-start(bf16[2,48,2304]{2,1,0:T(8,128)(2,1)S(1)} %get-tuple-element.220), channel_id=1, source_target_pairs={{0,2},{1,3},{2,0},{3,1},{4,6},{5,7},{6,4},{7,5},{8,10},{9,11},{10,... | collective-permute-start | bytes 1327112 | tf_op jit(solution)/shard_map/ppermute | solution.py:628
  99.2 22.4 %collective-permute-start.17 = (bf16[1,48,3072]{2,1,0:T(8,128)(2,1)S(1)}, bf16[1,48,3072]{2,1,0:T(8,128)(2,1)S(1)}, u32[]{:S(2)}, u32[]{:S(2)}) collective-permute-start(bf16[1,48,3072]{2,1,0:T(8,128)(2,1)S(1)} %get-tuple-element.232), channel_id=1, source_target_pairs={{0,4},{1,5},{2,6},{3,7},{4,0},{5,1},{6,2},{7,3},{8,12},{9,13},{10,... | collective-permute-start | bytes 884744 | tf_op jit(solution)/shard_map/ppermute | solution.py:628
  100.6 28.6 %collective-permute-start.16 = (bf16[1,48,3072]{2,1,0:T(8,128)(2,1)S(1)}, bf16[1,48,3072]{2,1,0:T(8,128)(2,1)S(1)}, u32[]{:S(2)}, u32[]{:S(2)}) collective-permute-start(bf16[1,48,3072]{2,1,0:T(8,128)(2,1)S(1)} %get-tuple-element.229), channel_id=1, source_target_pairs={{0,4},{1,5},{2,6},{3,7},{4,0},{5,1},{6,2},{7,3},{8,12},{9,13},{10,... | collective-permute-start | bytes 884744 | tf_op jit(solution)/shard_map/ppermute | solution.py:628
  117.8 11.6 %collective-permute-start.15 = (bf16[4,48,896]{2,1,0:T(8,128)(2,1)S(1)}, bf16[4,48,896]{2,1,0:T(8,128)(2,1)S(1)}, u32[]{:S(2)}, u32[]{:S(2)}) collective-permute-start(bf16[4,48,896]{2,1,0:T(8,128)(2,1)S(1)} %get-tuple-element.227), channel_id=1, source_target_pairs={{0,2},{1,3},{2,0},{3,1},{4,6},{5,7},{6,4},{7,5},{8,10},{9,11},{10,... | collective-permute-start | bytes 1032200 | tf_op jit(solution)/shard_map/ppermute | solution.py:628
  118.9 18.5 %collective-permute-start.18 = (bf16[1,48,2304]{2,1,0:T(8,128)(2,1)S(1)}, bf16[1,48,2304]{2,1,0:T(8,128)(2,1)S(1)}, u32[]{:S(2)}, u32[]{:S(2)}) collective-permute-start(bf16[1,48,2304]{2,1,0:T(8,128)(2,1)S(1)} %get-tuple-element.239), channel_id=1, source_target_pairs={{0,4},{1,5},{2,6},{3,7},{4,0},{5,1},{6,2},{7,3},{8,12},{9,13},{10,... | collective-permute-start | bytes 663560 | tf_op jit(solution)/shard_map/ppermute | solution.py:628
  120.3 23.3 %collective-permute-start.14 = (bf16[1,48,2304]{2,1,0:T(8,128)(2,1)S(1)}, bf16[1,48,2304]{2,1,0:T(8,128)(2,1)S(1)}, u32[]{:S(2)}, u32[]{:S(2)}) collective-permute-start(bf16[1,48,2304]{2,1,0:T(8,128)(2,1)S(1)} %get-tuple-element.224), channel_id=1, source_target_pairs={{0,4},{1,5},{2,6},{3,7},{4,0},{5,1},{6,2},{7,3},{8,12},{9,13},{10,... | collective-permute-start | bytes 663560 | tf_op jit(solution)/shard_map/ppermute | solution.py:628
  129.4 14.4 %collective-permute-start.22 = (bf16[1,48,3072]{2,1,0:T(8,128)(2,1)S(1)}, bf16[1,48,3072]{2,1,0:T(8,128)(2,1)S(1)}, u32[]{:S(2)}, u32[]{:S(2)}) collective-permute-start(bf16[1,48,3072]{2,1,0:T(8,128)(2,1)S(1)} %get-tuple-element.250), channel_id=1, source_target_pairs={{0,8},{1,9},{2,10},{3,11},{4,12},{5,13},{6,14},{7,15},{8,0},{9,1},... | collective-permute-start | bytes 884744 | tf_op jit(solution)/shard_map/ppermute | solution.py:628
  129.5 18.9 %collective-permute-start.20 = (bf16[1,192,768]{2,1,0:T(8,128)(2,1)S(1)}, bf16[1,192,768]{2,1,0:T(8,128)(2,1)S(1)}, u32[]{:S(2)}, u32[]{:S(2)}) collective-permute-start(bf16[1,192,768]{2,1,0:T(8,128)(2,1)S(1)} %get-tuple-element.246), channel_id=1, source_target_pairs={{0,2},{1,3},{2,0},{3,1},{4,6},{5,7},{6,4},{7,5},{8,10},{9,11},{10,... | collective-permute-start | bytes 884744 | tf_op jit(solution)/shard_map/ppermute | solution.py:628
  130.7 17.0 %collective-permute-start.21 = (bf16[2,48,896]{2,1,0:T(8,128)(2,1)S(1)}, bf16[2,48,896]{2,1,0:T(8,128)(2,1)S(1)}, u32[]{:S(2)}, u32[]{:S(2)}) collective-permute-start(bf16[2,48,896]{2,1,0:T(8,128)(2,1)S(1)} %get-tuple-element.248), channel_id=1, source_target_pairs={{0,4},{1,5},{2,6},{3,7},{4,0},{5,1},{6,2},{7,3},{8,12},{9,13},{10,... | collective-permute-start | bytes 516104 | tf_op jit(solution)/shard_map/ppermute | solution.py:628
  143.7 11.1 %collective-permute-start.19 = (bf16[1,48,2304]{2,1,0:T(8,128)(2,1)S(1)}, bf16[1,48,2304]{2,1,0:T(8,128)(2,1)S(1)}, u32[]{:S(2)}, u32[]{:S(2)}) collective-permute-start(bf16[1,48,2304]{2,1,0:T(8,128)(2,1)S(1)} %get-tuple-element.243), channel_id=1, source_target_pairs={{0,8},{1,9},{2,10},{3,11},{4,12},{5,13},{6,14},{7,15},{8,0},{9,1},... | collective-permute-start | bytes 663560 | tf_op jit(solution)/shard_map/ppermute | solution.py:628
  147.7 8.0 %collective-permute-start.23 = (bf16[1,48,896]{2,1,0:T(8,128)(2,1)S(1)}, bf16[1,48,896]{2,1,0:T(8,128)(2,1)S(1)}, u32[]{:S(2)}, u32[]{:S(2)}) collective-permute-start(bf16[1,48,896]{2,1,0:T(8,128)(2,1)S(1)} %get-tuple-element.257), channel_id=1, source_target_pairs={{0,8},{1,9},{2,10},{3,11},{4,12},{5,13},{6,14},{7,15},{8,0},{9,1},... | collective-permute-start | bytes 258056 | tf_op jit(solution)/shard_map/ppermute | solution.py:628
